TPU v7x, 512 devices: a whole 4x4x16 slice. The times are simulated.
512 devices in a mesh: video: 8 (over z_lo), cache: 16 (over x, z_hi, core), head: 4 (over y).
Axes of the slice: x: 4, y: 4, z: 16 (z_hi: 2, z_lo: 8; z = z_hi * 8 + z_lo), core: 2. Of those that a mesh axis runs over, the one named last changes fastest.
Arguments:
- queries: bfloat16 [8192, 6144], P(('video', 'cache'), 'head'), parts along dimension 0, may hold values from -6 to 6
- group_keys: bfloat16 [8192, 6144], P(('video', 'cache'), 'head'), parts along dimension 0, may hold values from -6 to 6
- group_values: bfloat16 [8192, 6144], P(('video', 'cache'), 'head'), parts along dimension 0, may hold values from -6 to 6
- cache_keys: bfloat16 [65536, 6144], P(('video', 'cache'), 'head'), parts along dimension 0, may hold values from -6 to 6
- cache_values: bfloat16 [65536, 6144], P(('video', 'cache'), 'head'), parts along dimension 0, may hold values from -6 to 6
- block_mask: int32 [128, 64], P('video', 'cache'), parts along dimension 0, may hold values from 0 to 1, as said below
- gain: bfloat16 [6144], replicated, may hold values from 0.5 to 1.5
Outputs:
- normed: bfloat16 [8192, 6144], P(('video', 'cache', 'head')), parts along dimension 0
There are 8 independent parts, one for each index of `video`. A program takes and returns all parts, laid end to end along the dimension named above; an argument that names none is the same for every part. Nothing has to cross between parts.
Inputs may be any that keep to these rules, and one draw needn't show every extreme that they name: `block_mask`: each cache shard's 4 blocks have their own density of ones, from one in eight to seven in eight.
All inputs are finite; a program needn't handle non-finite values.
Results may differ from a plain program's by a relative error of at most 0.025.
Values may be sent and summed in bfloat16 or wider, within the bound.
No kernel may reach another device: no remote copies, remote signals or barrier semaphores. Data moves between devices by JAX's collectives and lax.ppermute only.
A program may use at most 128 MiB of HBM per device.

v0:
```python
import jax
import jax.numpy as jnp
from jax import lax
from jax.sharding import PartitionSpec as P

HEAD_DIM = 128
BLOCK = 128


NEG = -1e30


def from_behind(block, axis, distance):
    devices = range(lax.axis_size(axis))
    route = [((i - distance) % len(devices), i) for i in devices]
    return lax.ppermute(block, axis, route)


def block_update(state, query_rows, keys, values, visible):
    running_max, denominator, numerator = state
    scale = HEAD_DIM ** (-0.5)
    scores = (
        jnp.einsum("qhd,khd->hqk", query_rows, keys, preferred_element_type=jnp.float32) * scale
    )
    scores = jnp.where(visible[None, None, :], scores, NEG)
    new_max = jnp.maximum(running_max, jnp.max(scores, axis=-1))
    weights = jnp.where(visible[None, None, :], jnp.exp(scores - new_max[:, :, None]), 0.0)
    factor = jnp.exp(running_max - new_max)
    denominator = denominator * factor + jnp.sum(weights, axis=-1)
    product = jnp.einsum(
        "hqk,khd->qhd", weights.astype(jnp.bfloat16), values, preferred_element_type=jnp.float32
    )
    numerator = numerator * jnp.transpose(factor)[:, :, None] + product
    return (new_max, denominator, numerator)


def attend_cache(state, query_rows, keys, values, mask_row):
    visible = jnp.repeat(mask_row > 0, BLOCK)
    return block_update(state, query_rows, keys, values, visible)


def local(queries, group_keys, group_values, cache_keys, cache_values, block_mask, gain):
    q_rows, features = queries.shape
    heads_here = features // HEAD_DIM
    query_rows = queries.reshape(q_rows, heads_here, HEAD_DIM)
    own_keys = group_keys.reshape(q_rows, heads_here, HEAD_DIM)
    own_values = group_values.reshape(q_rows, heads_here, HEAD_DIM)
    cached_keys = cache_keys.reshape(cache_keys.shape[0], heads_here, HEAD_DIM)
    cached_values = cache_values.reshape(cache_values.shape[0], heads_here, HEAD_DIM)
    empty_state = (
        jnp.full((heads_here, q_rows), NEG, jnp.float32),
        jnp.zeros((heads_here, q_rows), jnp.float32),
        jnp.zeros((q_rows, heads_here, HEAD_DIM), jnp.float32),
    )
    state = block_update(
        empty_state, query_rows, own_keys, own_values, jnp.ones((q_rows,), jnp.bool_)
    )
    count = lax.axis_size("cache")
    here = lax.axis_index("cache")

    def one_turn(step, carried):
        packet, current = carried
        tile_index = (here - step) % count
        mask_row = lax.dynamic_index_in_dim(block_mask, tile_index, 0, keepdims=False)
        current = attend_cache(
            current,
            packet.reshape(q_rows, heads_here, HEAD_DIM),
            cached_keys,
            cached_values,
            mask_row,
        )
        packet = from_behind(packet, "cache", 1)
        run_max, run_den, run_num = from_behind(
            (current[0], current[1], current[2].reshape(q_rows, features)), "cache", 1
        )
        return (packet, (run_max, run_den, run_num.reshape(q_rows, heads_here, HEAD_DIM)))

    _, state = lax.fori_loop(0, count, one_turn, (queries, state))
    final_max, final_den, final_num = state
    attended = (
        (final_num / jnp.transpose(final_den)[:, :, None])
        .astype(jnp.bfloat16)
        .reshape(q_rows, features)
    )
    token_rows = lax.all_to_all(attended, "head", split_axis=0, concat_axis=1, tiled=True)
    rows_float = token_rows.astype(jnp.float32)
    square_mean = jnp.mean(rows_float * rows_float, axis=-1, keepdims=True)
    normed = rows_float * lax.rsqrt(square_mean + 1e-06) * gain.astype(jnp.float32)
    return normed.astype(jnp.bfloat16)


def solution(mesh):
    in_specs = (
        P(("video", "cache"), "head"),
        P(("video", "cache"), "head"),
        P(("video", "cache"), "head"),
        P(("video", "cache"), "head"),
        P(("video", "cache"), "head"),
        P("video", "cache"),
        P(),
    )
    out_specs = P(("video", "cache", "head"), None)
    return jax.shard_map(local, mesh=mesh, in_specs=in_specs, out_specs=out_specs, check_vma=False)
```

profile of v0, /device:TPU:32, one launch (start us, length us, event | category | flops | bytes accessed | tf_op | source)
XLA Modules:
  0.0 689.3 jit_solution(5075909940762088211)
XLA Ops:
  12.8 653.4 %while.21 = (s32[]{:T(128)}, bf16[64,1536]{1,0:T(8,128)(2,1)}, f32[12,64]{1,0:T(8,128)S(1)}, f32[12,64]{1,0:T(8,128)}, f32[64,12,128]{2,1,0:T(8,128)}, /*index=5...) while((s32[]{:T(128)}, bf16[64,1536]{1,0:T(8,128)(2,1)}, ...), condition=%wide.region_5.6_spmd, body=%wide.region_2.5_spmd.sunk | while | flops 205064464 | bytes 14821872 | solution.py:78
  17.2 14.9 %collective-permute-start.1 = (f32[12,64]{1,0:T(8,128)S(1)}, f32[12,64]{1,0:T(8,128)}, u32[]{:S(2)}, u32[]{:S(2)}) collective-permute-start(f32[12,64]{1,0:T(8,128)S(1)} %get-tuple-element.342), channel_id=1, source_target_pairs={{60,0},{0,4},{4,8},{8,12},{12,16},{16,20},{20,24},{24,28},{28,32},... | collective-permute-start | bytes 9224 | tf_op jit(solution)/shard_map/while/body/eval_jaxpr/ppermute | solution.py:16
  40.0 25.7 %collective-permute-done.3 = f32[64,1536]{1,0:T(8,128)} collective-permute-done((f32[64,1536]{1,0:T(8,128)}, f32[64,1536]{1,0:T(8,128)}, u32[]{:S(2)}, u32[]{:S(2)}) %collective-permute-start.3) | collective-permute-done | bytes 393248 | tf_op jit(solution)/shard_map/while/body/eval_jaxpr/ppermute | solution.py:16
  79.0 10.5 %collective-permute-start.2 = (f32[12,64]{1,0:T(8,128)}, f32[12,64]{1,0:T(8,128)}, u32[]{:S(2)}, u32[]{:S(2)}) collective-permute-start(f32[12,64]{1,0:T(8,128)} %multiply_add_fusion.2), channel_id=1, source_target_pairs={{60,0},{0,4},{4,8},{8,12},{12,16},{16,20},{20,24},{24,28},{28,32},... | collective-permute-start | bytes 9224 | tf_op jit(solution)/shard_map/while/body/eval_jaxpr/ppermute | solution.py:16
  90.2 18.2 %collective-permute-done.3 = f32[64,1536]{1,0:T(8,128)} collective-permute-done((f32[64,1536]{1,0:T(8,128)}, f32[64,1536]{1,0:T(8,128)}, u32[]{:S(2)}, u32[]{:S(2)}) %collective-permute-start.3) | collective-permute-done | bytes 393248 | tf_op jit(solution)/shard_map/while/body/eval_jaxpr/ppermute | solution.py:16
  114.6 6.7 collective-permute-start.1
  126.5 8.2 %collective-permute-start.2 = (f32[12,64]{1,0:T(8,128)}, f32[12,64]{1,0:T(8,128)}, u32[]{:S(2)}, u32[]{:S(2)}) collective-permute-start(f32[12,64]{1,0:T(8,128)} %multiply_add_fusion.2), channel_id=1, source_target_pairs={{60,0},{0,4},{4,8},{8,12},{12,16},{16,20},{20,24},{24,28},{28,32},... | collective-permute-start | bytes 9224 | tf_op jit(solution)/shard_map/while/body/eval_jaxpr/ppermute | solution.py:16
  135.4 15.9 %collective-permute-done.3 = f32[64,1536]{1,0:T(8,128)} collective-permute-done((f32[64,1536]{1,0:T(8,128)}, f32[64,1536]{1,0:T(8,128)}, u32[]{:S(2)}, u32[]{:S(2)}) %collective-permute-start.3) | collective-permute-done | bytes 393248 | tf_op jit(solution)/shard_map/while/body/eval_jaxpr/ppermute | solution.py:16
  157.6 3.8 collective-permute-start.1
  166.5 9.7 %collective-permute-start.2 = (f32[12,64]{1,0:T(8,128)}, f32[12,64]{1,0:T(8,128)}, u32[]{:S(2)}, u32[]{:S(2)}) collective-permute-start(f32[12,64]{1,0:T(8,128)} %multiply_add_fusion.2), channel_id=1, source_target_pairs={{60,0},{0,4},{4,8},{8,12},{12,16},{16,20},{20,24},{24,28},{28,32},... | collective-permute-start | bytes 9224 | tf_op jit(solution)/shard_map/while/body/eval_jaxpr/ppermute | solution.py:16
  176.9 12.5 %collective-permute-done.3 = f32[64,1536]{1,0:T(8,128)} collective-permute-done((f32[64,1536]{1,0:T(8,128)}, f32[64,1536]{1,0:T(8,128)}, u32[]{:S(2)}, u32[]{:S(2)}) %collective-permute-start.3) | collective-permute-done | bytes 393248 | tf_op jit(solution)/shard_map/while/body/eval_jaxpr/ppermute | solution.py:16
  203.3 9.7 %collective-permute-start.2 = (f32[12,64]{1,0:T(8,128)}, f32[12,64]{1,0:T(8,128)}, u32[]{:S(2)}, u32[]{:S(2)}) collective-permute-start(f32[12,64]{1,0:T(8,128)} %multiply_add_fusion.2), channel_id=1, source_target_pairs={{60,0},{0,4},{4,8},{8,12},{12,16},{16,20},{20,24},{24,28},{28,32},... | collective-permute-start | bytes 9224 | tf_op jit(solution)/shard_map/while/body/eval_jaxpr/ppermute | solution.py:16
  215.7 8.4 %collective-permute-done.3 = f32[64,1536]{1,0:T(8,128)} collective-permute-done((f32[64,1536]{1,0:T(8,128)}, f32[64,1536]{1,0:T(8,128)}, u32[]{:S(2)}, u32[]{:S(2)}) %collective-permute-start.3) | collective-permute-done | bytes 393248 | tf_op jit(solution)/shard_map/while/body/eval_jaxpr/ppermute | solution.py:16
  230.3 6.3 collective-permute-start.1
  241.8 6.9 %collective-permute-start.2 = (f32[12,64]{1,0:T(8,128)}, f32[12,64]{1,0:T(8,128)}, u32[]{:S(2)}, u32[]{:S(2)}) collective-permute-start(f32[12,64]{1,0:T(8,128)} %multiply_add_fusion.2), channel_id=1, source_target_pairs={{60,0},{0,4},{4,8},{8,12},{12,16},{16,20},{20,24},{24,28},{28,32},... | collective-permute-start | bytes 9224 | tf_op jit(solution)/shard_map/while/body/eval_jaxpr/ppermute | solution.py:16
  249.5 13.0 %collective-permute-done.3 = f32[64,1536]{1,0:T(8,128)} collective-permute-done((f32[64,1536]{1,0:T(8,128)}, f32[64,1536]{1,0:T(8,128)}, u32[]{:S(2)}, u32[]{:S(2)}) %collective-permute-start.3) | collective-permute-done | bytes 393248 | tf_op jit(solution)/shard_map/while/body/eval_jaxpr/ppermute | solution.py:16
  268.8 5.2 collective-permute-start.1
  279.1 10.7 %collective-permute-start.2 = (f32[12,64]{1,0:T(8,128)}, f32[12,64]{1,0:T(8,128)}, u32[]{:S(2)}, u32[]{:S(2)}) collective-permute-start(f32[12,64]{1,0:T(8,128)} %multiply_add_fusion.2), channel_id=1, source_target_pairs={{60,0},{0,4},{4,8},{8,12},{12,16},{16,20},{20,24},{24,28},{28,32},... | collective-permute-start | bytes 9224 | tf_op jit(solution)/shard_map/while/body/eval_jaxpr/ppermute | solution.py:16
  290.6 8.0 %collective-permute-done.3 = f32[64,1536]{1,0:T(8,128)} collective-permute-done((f32[64,1536]{1,0:T(8,128)}, f32[64,1536]{1,0:T(8,128)}, u32[]{:S(2)}, u32[]{:S(2)}) %collective-permute-start.3) | collective-permute-done | bytes 393248 | tf_op jit(solution)/shard_map/while/body/eval_jaxpr/ppermute | solution.py:16
  304.9 10.3 %collective-permute-start.1 = (f32[12,64]{1,0:T(8,128)S(1)}, f32[12,64]{1,0:T(8,128)}, u32[]{:S(2)}, u32[]{:S(2)}) collective-permute-start(f32[12,64]{1,0:T(8,128)S(1)} %get-tuple-element.342), channel_id=1, source_target_pairs={{60,0},{0,4},{4,8},{8,12},{12,16},{16,20},{20,24},{24,28},{28,32},... | collective-permute-start | bytes 9224 | tf_op jit(solution)/shard_map/while/body/eval_jaxpr/ppermute | solution.py:16
  316.6 7.5 %collective-permute-start.3 = (f32[64,1536]{1,0:T(8,128)}, f32[64,1536]{1,0:T(8,128)}, u32[]{:S(2)}, u32[]{:S(2)}) collective-permute-start(f32[64,1536]{1,0:T(8,128)} %bitcast.85), channel_id=1, source_target_pairs={{60,0},{0,4},{4,8},{8,12},{12,16},{16,20},{20,24},{24,28},{28,32},... | collective-permute-start | bytes 1179656 | tf_op jit(solution)/shard_map/while/body/eval_jaxpr/ppermute | solution.py:16
  325.9 14.3 %collective-permute-start.2 = (f32[12,64]{1,0:T(8,128)}, f32[12,64]{1,0:T(8,128)}, u32[]{:S(2)}, u32[]{:S(2)}) collective-permute-start(f32[12,64]{1,0:T(8,128)} %multiply_add_fusion.2), channel_id=1, source_target_pairs={{60,0},{0,4},{4,8},{8,12},{12,16},{16,20},{20,24},{24,28},{28,32},... | collective-permute-start | bytes 9224 | tf_op jit(solution)/shard_map/while/body/eval_jaxpr/ppermute | solution.py:16
  343.8 11.2 %collective-permute-start = (bf16[64,1536]{1,0:T(8,128)(2,1)S(1)}, bf16[64,1536]{1,0:T(8,128)(2,1)}, u32[]{:S(2)}, u32[]{:S(2)}) collective-permute-start(bf16[64,1536]{1,0:T(8,128)(2,1)S(1)} %copy.93), channel_id=1, source_target_pairs={{60,0},{0,4},{4,8},{8,12},{12,16},{16,20},{20,24},{24,28},{28,32},... | collective-permute-start | bytes 589832 | tf_op jit(solution)/shard_map/while/body/eval_jaxpr/ppermute | solution.py:16
  356.6 14.6 %collective-permute-start.1 = (f32[12,64]{1,0:T(8,128)S(1)}, f32[12,64]{1,0:T(8,128)}, u32[]{:S(2)}, u32[]{:S(2)}) collective-permute-start(f32[12,64]{1,0:T(8,128)S(1)} %get-tuple-element.342), channel_id=1, source_target_pairs={{60,0},{0,4},{4,8},{8,12},{12,16},{16,20},{20,24},{24,28},{28,32},... | collective-permute-start | bytes 9224 | tf_op jit(solution)/shard_map/while/body/eval_jaxpr/ppermute | solution.py:16
  372.6 4.2 collective-permute-start.3
  378.7 14.1 %collective-permute-start.2 = (f32[12,64]{1,0:T(8,128)}, f32[12,64]{1,0:T(8,128)}, u32[]{:S(2)}, u32[]{:S(2)}) collective-permute-start(f32[12,64]{1,0:T(8,128)} %multiply_add_fusion.2), channel_id=1, source_target_pairs={{60,0},{0,4},{4,8},{8,12},{12,16},{16,20},{20,24},{24,28},{28,32},... | collective-permute-start | bytes 9224 | tf_op jit(solution)/shard_map/while/body/eval_jaxpr/ppermute | solution.py:16
  393.5 5.9 collective-permute-done.3
  405.7 13.2 %collective-permute-start.1 = (f32[12,64]{1,0:T(8,128)S(1)}, f32[12,64]{1,0:T(8,128)}, u32[]{:S(2)}, u32[]{:S(2)}) collective-permute-start(f32[12,64]{1,0:T(8,128)S(1)} %get-tuple-element.342), channel_id=1, source_target_pairs={{60,0},{0,4},{4,8},{8,12},{12,16},{16,20},{20,24},{24,28},{28,32},... | collective-permute-start | bytes 9224 | tf_op jit(solution)/shard_map/while/body/eval_jaxpr/ppermute | solution.py:16
  424.1 9.2 %collective-permute-start.2 = (f32[12,64]{1,0:T(8,128)}, f32[12,64]{1,0:T(8,128)}, u32[]{:S(2)}, u32[]{:S(2)}) collective-permute-start(f32[12,64]{1,0:T(8,128)} %multiply_add_fusion.2), channel_id=1, source_target_pairs={{60,0},{0,4},{4,8},{8,12},{12,16},{16,20},{20,24},{24,28},{28,32},... | collective-permute-start | bytes 9224 | tf_op jit(solution)/shard_map/while/body/eval_jaxpr/ppermute | solution.py:16
  434.0 9.9 %collective-permute-done.3 = f32[64,1536]{1,0:T(8,128)} collective-permute-done((f32[64,1536]{1,0:T(8,128)}, f32[64,1536]{1,0:T(8,128)}, u32[]{:S(2)}, u32[]{:S(2)}) %collective-permute-start.3) | collective-permute-done | bytes 393248 | tf_op jit(solution)/shard_map/while/body/eval_jaxpr/ppermute | solution.py:16
  450.2 6.5 collective-permute-start.1
  461.9 12.7 %collective-permute-start.2 = (f32[12,64]{1,0:T(8,128)}, f32[12,64]{1,0:T(8,128)}, u32[]{:S(2)}, u32[]{:S(2)}) collective-permute-start(f32[12,64]{1,0:T(8,128)} %multiply_add_fusion.2), channel_id=1, source_target_pairs={{60,0},{0,4},{4,8},{8,12},{12,16},{16,20},{20,24},{24,28},{28,32},... | collective-permute-start | bytes 9224 | tf_op jit(solution)/shard_map/while/body/eval_jaxpr/ppermute | solution.py:16
  476.4 3.6 collective-permute-done.3
  486.3 9.9 %collective-permute-start.1 = (f32[12,64]{1,0:T(8,128)S(1)}, f32[12,64]{1,0:T(8,128)}, u32[]{:S(2)}, u32[]{:S(2)}) collective-permute-start(f32[12,64]{1,0:T(8,128)S(1)} %get-tuple-element.342), channel_id=1, source_target_pairs={{60,0},{0,4},{4,8},{8,12},{12,16},{16,20},{20,24},{24,28},{28,32},... | collective-permute-start | bytes 9224 | tf_op jit(solution)/shard_map/while/body/eval_jaxpr/ppermute | solution.py:16
  501.4 12.2 %collective-permute-start.2 = (f32[12,64]{1,0:T(8,128)}, f32[12,64]{1,0:T(8,128)}, u32[]{:S(2)}, u32[]{:S(2)}) collective-permute-start(f32[12,64]{1,0:T(8,128)} %multiply_add_fusion.2), channel_id=1, source_target_pairs={{60,0},{0,4},{4,8},{8,12},{12,16},{16,20},{20,24},{24,28},{28,32},... | collective-permute-start | bytes 9224 | tf_op jit(solution)/shard_map/while/body/eval_jaxpr/ppermute | solution.py:16
  514.3 5.8 collective-permute-done.3
  526.4 12.5 %collective-permute-start.1 = (f32[12,64]{1,0:T(8,128)S(1)}, f32[12,64]{1,0:T(8,128)}, u32[]{:S(2)}, u32[]{:S(2)}) collective-permute-start(f32[12,64]{1,0:T(8,128)S(1)} %get-tuple-element.342), channel_id=1, source_target_pairs={{60,0},{0,4},{4,8},{8,12},{12,16},{16,20},{20,24},{24,28},{28,32},... | collective-permute-start | bytes 9224 | tf_op jit(solution)/shard_map/while/body/eval_jaxpr/ppermute | solution.py:16
  547.1 13.8 %collective-permute-done.3 = f32[64,1536]{1,0:T(8,128)} collective-permute-done((f32[64,1536]{1,0:T(8,128)}, f32[64,1536]{1,0:T(8,128)}, u32[]{:S(2)}, u32[]{:S(2)}) %collective-permute-start.3) | collective-permute-done | bytes 393248 | tf_op jit(solution)/shard_map/while/body/eval_jaxpr/ppermute | solution.py:16
  576.7 14.5 %collective-permute-done.1 = f32[12,64]{1,0:T(8,128)} collective-permute-done((f32[12,64]{1,0:T(8,128)S(1)}, f32[12,64]{1,0:T(8,128)}, u32[]{:S(2)}, u32[]{:S(2)}) %collective-permute-start.1) | collective-permute-done | bytes 3104 | tf_op jit(solution)/shard_map/while/body/eval_jaxpr/ppermute | solution.py:16
  591.9 3.7 collective-permute-done.3
  609.0 4.5 collective-permute-start.2
  613.5 11.1 %collective-permute-done.1 = f32[12,64]{1,0:T(8,128)} collective-permute-done((f32[12,64]{1,0:T(8,128)S(1)}, f32[12,64]{1,0:T(8,128)}, u32[]{:S(2)}, u32[]{:S(2)}) %collective-permute-start.1) | collective-permute-done | bytes 3104 | tf_op jit(solution)/shard_map/while/body/eval_jaxpr/ppermute | solution.py:16
  625.3 5.7 collective-permute-done.3
  644.4 7.2 %collective-permute-start.2 = (f32[12,64]{1,0:T(8,128)}, f32[12,64]{1,0:T(8,128)}, u32[]{:S(2)}, u32[]{:S(2)}) collective-permute-start(f32[12,64]{1,0:T(8,128)} %multiply_add_fusion.2), channel_id=1, source_target_pairs={{60,0},{0,4},{4,8},{8,12},{12,16},{16,20},{20,24},{24,28},{28,32},... | collective-permute-start | bytes 9224 | tf_op jit(solution)/shard_map/while/body/eval_jaxpr/ppermute | solution.py:16
  651.6 4.2 collective-permute-done.1
  656.5 7.9 %collective-permute-done.3 = f32[64,1536]{1,0:T(8,128)} collective-permute-done((f32[64,1536]{1,0:T(8,128)}, f32[64,1536]{1,0:T(8,128)}, u32[]{:S(2)}, u32[]{:S(2)}) %collective-permute-start.3) | collective-permute-done | bytes 393248 | tf_op jit(solution)/shard_map/while/body/eval_jaxpr/ppermute | solution.py:16
  669.1 12.9 %all-to-all-start = ((bf16[4,16,1536]{2,1,0:T(8,128)(2,1)}), bf16[4,16,1536]{2,1,0:T(8,128)(2,1)S(1)}, u32[]{:S(2)}, u32[]{:S(2)}) async-start(bf16[4,16,1536]{2,1,0:T(8,128)(2,1)} %all_to_all.10), calls=%async_computation | async-start | bytes 393216 | tf_op jit(solution)/shard_map/all_to_all | solution.py:85
  682.0 6.3 all-to-all-done
  (318 shorter events, 223.9 us)
Async XLA Ops:
  13.8 53.8 %collective-permute-start = (bf16[64,1536]{1,0:T(8,128)(2,1)S(1)}, bf16[64,1536]{1,0:T(8,128)(2,1)}, u32[]{:S(2)}, u32[]{:S(2)}) collective-permute-start(bf16[64,1536]{1,0:T(8,128)(2,1)S(1)} %copy.93), channel_id=1, source_target_pairs={{60,0},{0,4},{4,8},{8,12},{12,16},{16,20},{20,24},{24,28},{28,32},... | collective-permute-start | bytes 589832 | tf_op jit(solution)/shard_map/while/body/eval_jaxpr/ppermute | solution.py:16
  17.2 22.0 %collective-permute-start.1 = (f32[12,64]{1,0:T(8,128)S(1)}, f32[12,64]{1,0:T(8,128)}, u32[]{:S(2)}, u32[]{:S(2)}) collective-permute-start(f32[12,64]{1,0:T(8,128)S(1)} %get-tuple-element.342), channel_id=1, source_target_pairs={{60,0},{0,4},{4,8},{8,12},{12,16},{16,20},{20,24},{24,28},{28,32},... | collective-permute-start | bytes 9224 | tf_op jit(solution)/shard_map/while/body/eval_jaxpr/ppermute | solution.py:16
  33.6 32.0 %collective-permute-start.3 = (f32[64,1536]{1,0:T(8,128)}, f32[64,1536]{1,0:T(8,128)}, u32[]{:S(2)}, u32[]{:S(2)}) collective-permute-start(f32[64,1536]{1,0:T(8,128)} %bitcast.85), channel_id=1, source_target_pairs={{60,0},{0,4},{4,8},{8,12},{12,16},{16,20},{20,24},{24,28},{28,32},... | collective-permute-start | bytes 1179656 | tf_op jit(solution)/shard_map/while/body/eval_jaxpr/ppermute | solution.py:16
  37.3 30.2 %collective-permute-start.2 = (f32[12,64]{1,0:T(8,128)}, f32[12,64]{1,0:T(8,128)}, u32[]{:S(2)}, u32[]{:S(2)}) collective-permute-start(f32[12,64]{1,0:T(8,128)} %multiply_add_fusion.2), channel_id=1, source_target_pairs={{60,0},{0,4},{4,8},{8,12},{12,16},{16,20},{20,24},{24,28},{28,32},... | collective-permute-start | bytes 9224 | tf_op jit(solution)/shard_map/while/body/eval_jaxpr/ppermute | solution.py:16
  68.5 41.8 %collective-permute-start = (bf16[64,1536]{1,0:T(8,128)(2,1)S(1)}, bf16[64,1536]{1,0:T(8,128)(2,1)}, u32[]{:S(2)}, u32[]{:S(2)}) collective-permute-start(bf16[64,1536]{1,0:T(8,128)(2,1)S(1)} %copy.93), channel_id=1, source_target_pairs={{60,0},{0,4},{4,8},{8,12},{12,16},{16,20},{20,24},{24,28},{28,32},... | collective-permute-start | bytes 589832 | tf_op jit(solution)/shard_map/while/body/eval_jaxpr/ppermute | solution.py:16
  75.3 33.1 %collective-permute-start.3 = (f32[64,1536]{1,0:T(8,128)}, f32[64,1536]{1,0:T(8,128)}, u32[]{:S(2)}, u32[]{:S(2)}) collective-permute-start(f32[64,1536]{1,0:T(8,128)} %bitcast.85), channel_id=1, source_target_pairs={{60,0},{0,4},{4,8},{8,12},{12,16},{16,20},{20,24},{24,28},{28,32},... | collective-permute-start | bytes 1179656 | tf_op jit(solution)/shard_map/while/body/eval_jaxpr/ppermute | solution.py:16
  79.0 31.2 %collective-permute-start.2 = (f32[12,64]{1,0:T(8,128)}, f32[12,64]{1,0:T(8,128)}, u32[]{:S(2)}, u32[]{:S(2)}) collective-permute-start(f32[12,64]{1,0:T(8,128)} %multiply_add_fusion.2), channel_id=1, source_target_pairs={{60,0},{0,4},{4,8},{8,12},{12,16},{16,20},{20,24},{24,28},{28,32},... | collective-permute-start | bytes 9224 | tf_op jit(solution)/shard_map/while/body/eval_jaxpr/ppermute | solution.py:16
  111.2 42.0 %collective-permute-start = (bf16[64,1536]{1,0:T(8,128)(2,1)S(1)}, bf16[64,1536]{1,0:T(8,128)(2,1)}, u32[]{:S(2)}, u32[]{:S(2)}) collective-permute-start(bf16[64,1536]{1,0:T(8,128)(2,1)S(1)} %copy.93), channel_id=1, source_target_pairs={{60,0},{0,4},{4,8},{8,12},{12,16},{16,20},{20,24},{24,28},{28,32},... | collective-permute-start | bytes 589832 | tf_op jit(solution)/shard_map/while/body/eval_jaxpr/ppermute | solution.py:16
  122.8 28.5 %collective-permute-start.3 = (f32[64,1536]{1,0:T(8,128)}, f32[64,1536]{1,0:T(8,128)}, u32[]{:S(2)}, u32[]{:S(2)}) collective-permute-start(f32[64,1536]{1,0:T(8,128)} %bitcast.85), channel_id=1, source_target_pairs={{60,0},{0,4},{4,8},{8,12},{12,16},{16,20},{20,24},{24,28},{28,32},... | collective-permute-start | bytes 1179656 | tf_op jit(solution)/shard_map/while/body/eval_jaxpr/ppermute | solution.py:16
  126.5 26.7 %collective-permute-start.2 = (f32[12,64]{1,0:T(8,128)}, f32[12,64]{1,0:T(8,128)}, u32[]{:S(2)}, u32[]{:S(2)}) collective-permute-start(f32[12,64]{1,0:T(8,128)} %multiply_add_fusion.2), channel_id=1, source_target_pairs={{60,0},{0,4},{4,8},{8,12},{12,16},{16,20},{20,24},{24,28},{28,32},... | collective-permute-start | bytes 9224 | tf_op jit(solution)/shard_map/while/body/eval_jaxpr/ppermute | solution.py:16
  154.1 37.2 %collective-permute-start = (bf16[64,1536]{1,0:T(8,128)(2,1)S(1)}, bf16[64,1536]{1,0:T(8,128)(2,1)}, u32[]{:S(2)}, u32[]{:S(2)}) collective-permute-start(bf16[64,1536]{1,0:T(8,128)(2,1)S(1)} %copy.93), channel_id=1, source_target_pairs={{60,0},{0,4},{4,8},{8,12},{12,16},{16,20},{20,24},{24,28},{28,32},... | collective-permute-start | bytes 589832 | tf_op jit(solution)/shard_map/while/body/eval_jaxpr/ppermute | solution.py:16
  162.8 26.7 %collective-permute-start.3 = (f32[64,1536]{1,0:T(8,128)}, f32[64,1536]{1,0:T(8,128)}, u32[]{:S(2)}, u32[]{:S(2)}) collective-permute-start(f32[64,1536]{1,0:T(8,128)} %bitcast.85), channel_id=1, source_target_pairs={{60,0},{0,4},{4,8},{8,12},{12,16},{16,20},{20,24},{24,28},{28,32},... | collective-permute-start | bytes 1179656 | tf_op jit(solution)/shard_map/while/body/eval_jaxpr/ppermute | solution.py:16
  166.5 24.8 %collective-permute-start.2 = (f32[12,64]{1,0:T(8,128)}, f32[12,64]{1,0:T(8,128)}, u32[]{:S(2)}, u32[]{:S(2)}) collective-permute-start(f32[12,64]{1,0:T(8,128)} %multiply_add_fusion.2), channel_id=1, source_target_pairs={{60,0},{0,4},{4,8},{8,12},{12,16},{16,20},{20,24},{24,28},{28,32},... | collective-permute-start | bytes 9224 | tf_op jit(solution)/shard_map/while/body/eval_jaxpr/ppermute | solution.py:16
  192.2 33.7 %collective-permute-start = (bf16[64,1536]{1,0:T(8,128)(2,1)S(1)}, bf16[64,1536]{1,0:T(8,128)(2,1)}, u32[]{:S(2)}, u32[]{:S(2)}) collective-permute-start(bf16[64,1536]{1,0:T(8,128)(2,1)S(1)} %copy.93), channel_id=1, source_target_pairs={{60,0},{0,4},{4,8},{8,12},{12,16},{16,20},{20,24},{24,28},{28,32},... | collective-permute-start | bytes 589832 | tf_op jit(solution)/shard_map/while/body/eval_jaxpr/ppermute | solution.py:16
  199.6 24.5 %collective-permute-start.3 = (f32[64,1536]{1,0:T(8,128)}, f32[64,1536]{1,0:T(8,128)}, u32[]{:S(2)}, u32[]{:S(2)}) collective-permute-start(f32[64,1536]{1,0:T(8,128)} %bitcast.85), channel_id=1, source_target_pairs={{60,0},{0,4},{4,8},{8,12},{12,16},{16,20},{20,24},{24,28},{28,32},... | collective-permute-start | bytes 1179656 | tf_op jit(solution)/shard_map/while/body/eval_jaxpr/ppermute | solution.py:16
  203.3 22.6 %collective-permute-start.2 = (f32[12,64]{1,0:T(8,128)}, f32[12,64]{1,0:T(8,128)}, u32[]{:S(2)}, u32[]{:S(2)}) collective-permute-start(f32[12,64]{1,0:T(8,128)} %multiply_add_fusion.2), channel_id=1, source_target_pairs={{60,0},{0,4},{4,8},{8,12},{12,16},{16,20},{20,24},{24,28},{28,32},... | collective-permute-start | bytes 9224 | tf_op jit(solution)/shard_map/while/body/eval_jaxpr/ppermute | solution.py:16
  226.9 37.5 %collective-permute-start = (bf16[64,1536]{1,0:T(8,128)(2,1)S(1)}, bf16[64,1536]{1,0:T(8,128)(2,1)}, u32[]{:S(2)}, u32[]{:S(2)}) collective-permute-start(bf16[64,1536]{1,0:T(8,128)(2,1)S(1)} %copy.93), channel_id=1, source_target_pairs={{60,0},{0,4},{4,8},{8,12},{12,16},{16,20},{20,24},{24,28},{28,32},... | collective-permute-start | bytes 589832 | tf_op jit(solution)/shard_map/while/body/eval_jaxpr/ppermute | solution.py:16
  238.1 24.4 %collective-permute-start.3 = (f32[64,1536]{1,0:T(8,128)}, f32[64,1536]{1,0:T(8,128)}, u32[]{:S(2)}, u32[]{:S(2)}) collective-permute-start(f32[64,1536]{1,0:T(8,128)} %bitcast.85), channel_id=1, source_target_pairs={{60,0},{0,4},{4,8},{8,12},{12,16},{16,20},{20,24},{24,28},{28,32},... | collective-permute-start | bytes 1179656 | tf_op jit(solution)/shard_map/while/body/eval_jaxpr/ppermute | solution.py:16
  241.8 22.6 %collective-permute-start.2 = (f32[12,64]{1,0:T(8,128)}, f32[12,64]{1,0:T(8,128)}, u32[]{:S(2)}, u32[]{:S(2)}) collective-permute-start(f32[12,64]{1,0:T(8,128)} %multiply_add_fusion.2), channel_id=1, source_target_pairs={{60,0},{0,4},{4,8},{8,12},{12,16},{16,20},{20,24},{24,28},{28,32},... | collective-permute-start | bytes 9224 | tf_op jit(solution)/shard_map/while/body/eval_jaxpr/ppermute | solution.py:16
  265.3 35.2 %collective-permute-start = (bf16[64,1536]{1,0:T(8,128)(2,1)S(1)}, bf16[64,1536]{1,0:T(8,128)(2,1)}, u32[]{:S(2)}, u32[]{:S(2)}) collective-permute-start(bf16[64,1536]{1,0:T(8,128)(2,1)S(1)} %copy.93), channel_id=1, source_target_pairs={{60,0},{0,4},{4,8},{8,12},{12,16},{16,20},{20,24},{24,28},{28,32},... | collective-permute-start | bytes 589832 | tf_op jit(solution)/shard_map/while/body/eval_jaxpr/ppermute | solution.py:16
  275.4 23.2 %collective-permute-start.3 = (f32[64,1536]{1,0:T(8,128)}, f32[64,1536]{1,0:T(8,128)}, u32[]{:S(2)}, u32[]{:S(2)}) collective-permute-start(f32[64,1536]{1,0:T(8,128)} %bitcast.85), channel_id=1, source_target_pairs={{60,0},{0,4},{4,8},{8,12},{12,16},{16,20},{20,24},{24,28},{28,32},... | collective-permute-start | bytes 1179656 | tf_op jit(solution)/shard_map/while/body/eval_jaxpr/ppermute | solution.py:16
  301.4 41.4 %collective-permute-start = (bf16[64,1536]{1,0:T(8,128)(2,1)S(1)}, bf16[64,1536]{1,0:T(8,128)(2,1)}, u32[]{:S(2)}, u32[]{:S(2)}) collective-permute-start(bf16[64,1536]{1,0:T(8,128)(2,1)S(1)} %copy.93), channel_id=1, source_target_pairs={{60,0},{0,4},{4,8},{8,12},{12,16},{16,20},{20,24},{24,28},{28,32},... | collective-permute-start | bytes 589832 | tf_op jit(solution)/shard_map/while/body/eval_jaxpr/ppermute | solution.py:16
  304.9 35.3 %collective-permute-start.1 = (f32[12,64]{1,0:T(8,128)S(1)}, f32[12,64]{1,0:T(8,128)}, u32[]{:S(2)}, u32[]{:S(2)}) collective-permute-start(f32[12,64]{1,0:T(8,128)S(1)} %get-tuple-element.342), channel_id=1, source_target_pairs={{60,0},{0,4},{4,8},{8,12},{12,16},{16,20},{20,24},{24,28},{28,32},... | collective-permute-start | bytes 9224 | tf_op jit(solution)/shard_map/while/body/eval_jaxpr/ppermute | solution.py:16
  316.6 24.4 %collective-permute-start.3 = (f32[64,1536]{1,0:T(8,128)}, f32[64,1536]{1,0:T(8,128)}, u32[]{:S(2)}, u32[]{:S(2)}) collective-permute-start(f32[64,1536]{1,0:T(8,128)} %bitcast.85), channel_id=1, source_target_pairs={{60,0},{0,4},{4,8},{8,12},{12,16},{16,20},{20,24},{24,28},{28,32},... | collective-permute-start | bytes 1179656 | tf_op jit(solution)/shard_map/while/body/eval_jaxpr/ppermute | solution.py:16
  343.8 57.5 %collective-permute-start = (bf16[64,1536]{1,0:T(8,128)(2,1)S(1)}, bf16[64,1536]{1,0:T(8,128)(2,1)}, u32[]{:S(2)}, u32[]{:S(2)}) collective-permute-start(bf16[64,1536]{1,0:T(8,128)(2,1)S(1)} %copy.93), channel_id=1, source_target_pairs={{60,0},{0,4},{4,8},{8,12},{12,16},{16,20},{20,24},{24,28},{28,32},... | collective-permute-start | bytes 589832 | tf_op jit(solution)/shard_map/while/body/eval_jaxpr/ppermute | solution.py:16
  356.6 36.2 %collective-permute-start.1 = (f32[12,64]{1,0:T(8,128)S(1)}, f32[12,64]{1,0:T(8,128)}, u32[]{:S(2)}, u32[]{:S(2)}) collective-permute-start(f32[12,64]{1,0:T(8,128)S(1)} %get-tuple-element.342), channel_id=1, source_target_pairs={{60,0},{0,4},{4,8},{8,12},{12,16},{16,20},{20,24},{24,28},{28,32},... | collective-permute-start | bytes 9224 | tf_op jit(solution)/shard_map/while/body/eval_jaxpr/ppermute | solution.py:16
  372.6 26.8 %collective-permute-start.3 = (f32[64,1536]{1,0:T(8,128)}, f32[64,1536]{1,0:T(8,128)}, u32[]{:S(2)}, u32[]{:S(2)}) collective-permute-start(f32[64,1536]{1,0:T(8,128)} %bitcast.85), channel_id=1, source_target_pairs={{60,0},{0,4},{4,8},{8,12},{12,16},{16,20},{20,24},{24,28},{28,32},... | collective-permute-start | bytes 1179656 | tf_op jit(solution)/shard_map/while/body/eval_jaxpr/ppermute | solution.py:16
  378.7 22.6 %collective-permute-start.2 = (f32[12,64]{1,0:T(8,128)}, f32[12,64]{1,0:T(8,128)}, u32[]{:S(2)}, u32[]{:S(2)}) collective-permute-start(f32[12,64]{1,0:T(8,128)} %multiply_add_fusion.2), channel_id=1, source_target_pairs={{60,0},{0,4},{4,8},{8,12},{12,16},{16,20},{20,24},{24,28},{28,32},... | collective-permute-start | bytes 9224 | tf_op jit(solution)/shard_map/while/body/eval_jaxpr/ppermute | solution.py:16
  402.2 43.6 %collective-permute-start = (bf16[64,1536]{1,0:T(8,128)(2,1)S(1)}, bf16[64,1536]{1,0:T(8,128)(2,1)}, u32[]{:S(2)}, u32[]{:S(2)}) collective-permute-start(bf16[64,1536]{1,0:T(8,128)(2,1)S(1)} %copy.93), channel_id=1, source_target_pairs={{60,0},{0,4},{4,8},{8,12},{12,16},{16,20},{20,24},{24,28},{28,32},... | collective-permute-start | bytes 589832 | tf_op jit(solution)/shard_map/while/body/eval_jaxpr/ppermute | solution.py:16
  405.7 27.6 %collective-permute-start.1 = (f32[12,64]{1,0:T(8,128)S(1)}, f32[12,64]{1,0:T(8,128)}, u32[]{:S(2)}, u32[]{:S(2)}) collective-permute-start(f32[12,64]{1,0:T(8,128)S(1)} %get-tuple-element.342), channel_id=1, source_target_pairs={{60,0},{0,4},{4,8},{8,12},{12,16},{16,20},{20,24},{24,28},{28,32},... | collective-permute-start | bytes 9224 | tf_op jit(solution)/shard_map/while/body/eval_jaxpr/ppermute | solution.py:16
  420.3 23.6 %collective-permute-start.3 = (f32[64,1536]{1,0:T(8,128)}, f32[64,1536]{1,0:T(8,128)}, u32[]{:S(2)}, u32[]{:S(2)}) collective-permute-start(f32[64,1536]{1,0:T(8,128)} %bitcast.85), channel_id=1, source_target_pairs={{60,0},{0,4},{4,8},{8,12},{12,16},{16,20},{20,24},{24,28},{28,32},... | collective-permute-start | bytes 1179656 | tf_op jit(solution)/shard_map/while/body/eval_jaxpr/ppermute | solution.py:16
  446.8 35.2 %collective-permute-start = (bf16[64,1536]{1,0:T(8,128)(2,1)S(1)}, bf16[64,1536]{1,0:T(8,128)(2,1)}, u32[]{:S(2)}, u32[]{:S(2)}) collective-permute-start(bf16[64,1536]{1,0:T(8,128)(2,1)S(1)} %copy.93), channel_id=1, source_target_pairs={{60,0},{0,4},{4,8},{8,12},{12,16},{16,20},{20,24},{24,28},{28,32},... | collective-permute-start | bytes 589832 | tf_op jit(solution)/shard_map/while/body/eval_jaxpr/ppermute | solution.py:16
  450.2 25.5 %collective-permute-start.1 = (f32[12,64]{1,0:T(8,128)S(1)}, f32[12,64]{1,0:T(8,128)}, u32[]{:S(2)}, u32[]{:S(2)}) collective-permute-start(f32[12,64]{1,0:T(8,128)S(1)} %get-tuple-element.342), channel_id=1, source_target_pairs={{60,0},{0,4},{4,8},{8,12},{12,16},{16,20},{20,24},{24,28},{28,32},... | collective-permute-start | bytes 9224 | tf_op jit(solution)/shard_map/while/body/eval_jaxpr/ppermute | solution.py:16
  458.2 21.9 %collective-permute-start.3 = (f32[64,1536]{1,0:T(8,128)}, f32[64,1536]{1,0:T(8,128)}, u32[]{:S(2)}, u32[]{:S(2)}) collective-permute-start(f32[64,1536]{1,0:T(8,128)} %bitcast.85), channel_id=1, source_target_pairs={{60,0},{0,4},{4,8},{8,12},{12,16},{16,20},{20,24},{24,28},{28,32},... | collective-permute-start | bytes 1179656 | tf_op jit(solution)/shard_map/while/body/eval_jaxpr/ppermute | solution.py:16
  482.9 39.2 %collective-permute-start = (bf16[64,1536]{1,0:T(8,128)(2,1)S(1)}, bf16[64,1536]{1,0:T(8,128)(2,1)}, u32[]{:S(2)}, u32[]{:S(2)}) collective-permute-start(bf16[64,1536]{1,0:T(8,128)(2,1)S(1)} %copy.93), channel_id=1, source_target_pairs={{60,0},{0,4},{4,8},{8,12},{12,16},{16,20},{20,24},{24,28},{28,32},... | collective-permute-start | bytes 589832 | tf_op jit(solution)/shard_map/while/body/eval_jaxpr/ppermute | solution.py:16
  486.3 27.3 %collective-permute-start.1 = (f32[12,64]{1,0:T(8,128)S(1)}, f32[12,64]{1,0:T(8,128)}, u32[]{:S(2)}, u32[]{:S(2)}) collective-permute-start(f32[12,64]{1,0:T(8,128)S(1)} %get-tuple-element.342), channel_id=1, source_target_pairs={{60,0},{0,4},{4,8},{8,12},{12,16},{16,20},{20,24},{24,28},{28,32},... | collective-permute-start | bytes 9224 | tf_op jit(solution)/shard_map/while/body/eval_jaxpr/ppermute | solution.py:16
  497.6 22.5 %collective-permute-start.3 = (f32[64,1536]{1,0:T(8,128)}, f32[64,1536]{1,0:T(8,128)}, u32[]{:S(2)}, u32[]{:S(2)}) collective-permute-start(f32[64,1536]{1,0:T(8,128)} %bitcast.85), channel_id=1, source_target_pairs={{60,0},{0,4},{4,8},{8,12},{12,16},{16,20},{20,24},{24,28},{28,32},... | collective-permute-start | bytes 1179656 | tf_op jit(solution)/shard_map/while/body/eval_jaxpr/ppermute | solution.py:16
  523.0 39.8 %collective-permute-start = (bf16[64,1536]{1,0:T(8,128)(2,1)S(1)}, bf16[64,1536]{1,0:T(8,128)(2,1)}, u32[]{:S(2)}, u32[]{:S(2)}) collective-permute-start(bf16[64,1536]{1,0:T(8,128)(2,1)S(1)} %copy.93), channel_id=1, source_target_pairs={{60,0},{0,4},{4,8},{8,12},{12,16},{16,20},{20,24},{24,28},{28,32},... | collective-permute-start | bytes 589832 | tf_op jit(solution)/shard_map/while/body/eval_jaxpr/ppermute | solution.py:16
  563.7 33.8 %collective-permute-start = (bf16[64,1536]{1,0:T(8,128)(2,1)S(1)}, bf16[64,1536]{1,0:T(8,128)(2,1)}, u32[]{:S(2)}, u32[]{:S(2)}) collective-permute-start(bf16[64,1536]{1,0:T(8,128)(2,1)S(1)} %copy.93), channel_id=1, source_target_pairs={{60,0},{0,4},{4,8},{8,12},{12,16},{16,20},{20,24},{24,28},{28,32},... | collective-permute-start | bytes 589832 | tf_op jit(solution)/shard_map/while/body/eval_jaxpr/ppermute | solution.py:16
  567.2 24.0 %collective-permute-start.1 = (f32[12,64]{1,0:T(8,128)S(1)}, f32[12,64]{1,0:T(8,128)}, u32[]{:S(2)}, u32[]{:S(2)}) collective-permute-start(f32[12,64]{1,0:T(8,128)S(1)} %get-tuple-element.342), channel_id=1, source_target_pairs={{60,0},{0,4},{4,8},{8,12},{12,16},{16,20},{20,24},{24,28},{28,32},... | collective-permute-start | bytes 9224 | tf_op jit(solution)/shard_map/while/body/eval_jaxpr/ppermute | solution.py:16
  570.5 25.1 %collective-permute-start.3 = (f32[64,1536]{1,0:T(8,128)}, f32[64,1536]{1,0:T(8,128)}, u32[]{:S(2)}, u32[]{:S(2)}) collective-permute-start(f32[64,1536]{1,0:T(8,128)} %bitcast.85), channel_id=1, source_target_pairs={{60,0},{0,4},{4,8},{8,12},{12,16},{16,20},{20,24},{24,28},{28,32},... | collective-permute-start | bytes 1179656 | tf_op jit(solution)/shard_map/while/body/eval_jaxpr/ppermute | solution.py:16
  574.3 23.3 %collective-permute-start.2 = (f32[12,64]{1,0:T(8,128)}, f32[12,64]{1,0:T(8,128)}, u32[]{:S(2)}, u32[]{:S(2)}) collective-permute-start(f32[12,64]{1,0:T(8,128)} %multiply_add_fusion.2), channel_id=1, source_target_pairs={{60,0},{0,4},{4,8},{8,12},{12,16},{16,20},{20,24},{24,28},{28,32},... | collective-permute-start | bytes 9224 | tf_op jit(solution)/shard_map/while/body/eval_jaxpr/ppermute | solution.py:16
  598.4 34.5 %collective-permute-start = (bf16[64,1536]{1,0:T(8,128)(2,1)S(1)}, bf16[64,1536]{1,0:T(8,128)(2,1)}, u32[]{:S(2)}, u32[]{:S(2)}) collective-permute-start(bf16[64,1536]{1,0:T(8,128)(2,1)S(1)} %copy.93), channel_id=1, source_target_pairs={{60,0},{0,4},{4,8},{8,12},{12,16},{16,20},{20,24},{24,28},{28,32},... | collective-permute-start | bytes 589832 | tf_op jit(solution)/shard_map/while/body/eval_jaxpr/ppermute | solution.py:16
  601.9 22.7 %collective-permute-start.1 = (f32[12,64]{1,0:T(8,128)S(1)}, f32[12,64]{1,0:T(8,128)}, u32[]{:S(2)}, u32[]{:S(2)}) collective-permute-start(f32[12,64]{1,0:T(8,128)S(1)} %get-tuple-element.342), channel_id=1, source_target_pairs={{60,0},{0,4},{4,8},{8,12},{12,16},{16,20},{20,24},{24,28},{28,32},... | collective-permute-start | bytes 9224 | tf_op jit(solution)/shard_map/while/body/eval_jaxpr/ppermute | solution.py:16
  605.3 25.8 %collective-permute-start.3 = (f32[64,1536]{1,0:T(8,128)}, f32[64,1536]{1,0:T(8,128)}, u32[]{:S(2)}, u32[]{:S(2)}) collective-permute-start(f32[64,1536]{1,0:T(8,128)} %bitcast.85), channel_id=1, source_target_pairs={{60,0},{0,4},{4,8},{8,12},{12,16},{16,20},{20,24},{24,28},{28,32},... | collective-permute-start | bytes 1179656 | tf_op jit(solution)/shard_map/while/body/eval_jaxpr/ppermute | solution.py:16
  609.0 23.9 %collective-permute-start.2 = (f32[12,64]{1,0:T(8,128)}, f32[12,64]{1,0:T(8,128)}, u32[]{:S(2)}, u32[]{:S(2)}) collective-permute-start(f32[12,64]{1,0:T(8,128)} %multiply_add_fusion.2), channel_id=1, source_target_pairs={{60,0},{0,4},{4,8},{8,12},{12,16},{16,20},{20,24},{24,28},{28,32},... | collective-permute-start | bytes 9224 | tf_op jit(solution)/shard_map/while/body/eval_jaxpr/ppermute | solution.py:16
  633.9 32.4 %collective-permute-start = (bf16[64,1536]{1,0:T(8,128)(2,1)S(1)}, bf16[64,1536]{1,0:T(8,128)(2,1)}, u32[]{:S(2)}, u32[]{:S(2)}) collective-permute-start(bf16[64,1536]{1,0:T(8,128)(2,1)S(1)} %copy.93), channel_id=1, source_target_pairs={{60,0},{0,4},{4,8},{8,12},{12,16},{16,20},{20,24},{24,28},{28,32},... | collective-permute-start | bytes 589832 | tf_op jit(solution)/shard_map/while/body/eval_jaxpr/ppermute | solution.py:16
  640.7 23.7 %collective-permute-start.3 = (f32[64,1536]{1,0:T(8,128)}, f32[64,1536]{1,0:T(8,128)}, u32[]{:S(2)}, u32[]{:S(2)}) collective-permute-start(f32[64,1536]{1,0:T(8,128)} %bitcast.85), channel_id=1, source_target_pairs={{60,0},{0,4},{4,8},{8,12},{12,16},{16,20},{20,24},{24,28},{28,32},... | collective-permute-start | bytes 1179656 | tf_op jit(solution)/shard_map/while/body/eval_jaxpr/ppermute | solution.py:16
  (36 other events, 482.0 us)
where the time goes:
time: 694 us; the launch traced here: 689 us
  starting transfers between devices  342 us (49%)
  waiting for transfers between devices  198 us (29%)
  local copies, waits for them, and re-layouts  81.9 us (12%)
  other arithmetic  43.2 us (6%)
  matrix products  23.4 us (3%)
    ppermute x64, starting transfers between devices, from_behind(): return lax.ppermute(block, axis, route)  329 us
    ppermute x64, waiting for transfers between devices, from_behind(): return lax.ppermute(block, axis, route)  191 us
    reshape x16, local copies, waits for them, and re-layouts, one_turn(): run_num.reshape(q_rows, heads_here, HEAD_DIM)  30 us
    add x16, other arithmetic, block_update(): denominator = denominator * factor + jnp.sum(weights, axis=-1)  20.9 us
    another operation x16, local copies, waits for them, and re-layouts  14.9 us
  transfers between devices with their start and end apart: 65, of which 23 were waited for; matrix products, arithmetic and copies ran while one was open for 17% of the time, Pallas kernels for 0%

commit v1 on v0

v1 whole, which is shorter than its diff:
```python
import jax
import jax.numpy as jnp
from jax import lax
from jax.experimental import pallas as pl
from jax.experimental.pallas import tpu as pltpu
from jax.sharding import Mesh
from jax.sharding import PartitionSpec as P

HEAD_DIM = 128
BLOCK = 128
HEADS_X = 3
Q_ROWS = 64
ROWS = 8 * Q_ROWS
TOK = 512
LOG2_SCALE = HEAD_DIM ** (-0.5) * 1.4426950408889634
NEG = -1e30
KEYS = slice(0, TOK)
VALUES = slice(TOK, 2 * TOK)
HIDDEN = slice(2 * TOK, 2 * TOK + 16)
OWN_KEYS = slice(2 * TOK + 16, 2 * TOK + 16 + Q_ROWS)
OWN_VALUES = slice(2 * TOK + 16 + Q_ROWS, 2 * TOK + 16 + 2 * Q_ROWS)
QUERIES = slice(2 * TOK + 16 + 2 * Q_ROWS, 2 * TOK + 16 + 3 * Q_ROWS)
PACKET = 2 * TOK + 16 + 3 * Q_ROWS
STATS = 8
NT = (((1,), (1,)), ((), ()))
NN = (((1,), (0,)), ((), ()))
VMEM = pl.BlockSpec(memory_space=pltpu.VMEM)
SMEM = pl.BlockSpec(memory_space=pltpu.SMEM)
PARAMS = pltpu.CompilerParams(vmem_limit_bytes=60 * 2**20)


def with_ones(values):
    return jnp.concatenate([values, jnp.ones((values.shape[0], HEAD_DIM), jnp.bfloat16)], 1)


def matmul(a, b, dims):
    return lax.dot_general(a, b, dims, preferred_element_type=jnp.float32)


def fold(scores, values, top, total):
    new_top = jnp.maximum(top, jnp.max(scores, axis=1, keepdims=True))
    weights = jnp.exp2((scores - new_top) * LOG2_SCALE).astype(jnp.bfloat16)
    factor = jnp.exp2((top - new_top) * LOG2_SCALE)
    return new_top, total * factor + matmul(weights, with_ones(values), NN)


def pack_kernel(k_ref, v_ref, mask_ref, own_k_ref, own_v_ref, q_ref, out_ref):
    hidden = jnp.where(mask_ref[...] > 0, 0.0, NEG)
    hidden = jnp.concatenate([hidden, jnp.zeros((16, HEAD_DIM - 4), jnp.float32)], 1)
    out_ref[0, KEYS, :] = k_ref[...]
    out_ref[0, VALUES, :] = v_ref[...]
    out_ref[0, HIDDEN, :] = jnp.concatenate([hidden.astype(jnp.bfloat16)] * HEADS_X, 1)
    out_ref[0, OWN_KEYS, :] = own_k_ref[...]
    out_ref[0, OWN_VALUES, :] = own_v_ref[...]
    out_ref[0, QUERIES, :] = q_ref[...]


def pack(keys, values, mask, own_keys, own_values, queries):
    width = HEADS_X * HEAD_DIM
    big = pl.BlockSpec((TOK, width), lambda x: (0, x))
    small = pl.BlockSpec((Q_ROWS, width), lambda x: (0, x))
    return pl.pallas_call(
        pack_kernel,
        grid=(4,),
        in_specs=[big, big, pl.BlockSpec((16, 4), lambda x: (0, 0)), small, small, small],
        out_specs=pl.BlockSpec((1, PACKET, width), lambda x: (x, 0, 0)),
        out_shape=jax.ShapeDtypeStruct((4, PACKET, width), jnp.bfloat16),
        compiler_params=PARAMS,
    )(keys, values, mask, own_keys, own_values, queries)


def attend_kernel(place_ref, *refs):
    far, (mine_ref, theirs_ref, out_ref, log_ref, logs_ref, hidden_ref, bias_ref) = refs[:4], refs[4:]
    head = pl.program_id(0)
    core, z = place_ref[4], place_ref[5]
    caches = (mine_ref, theirs_ref)
    where = [(t, z) if t < 4 else (place_ref[t - 4], 1 - z) for t in range(8)]

    @pl.when(head == 0)
    def _():
        for src in range(8):
            hidden_ref[src] = caches[src % 2][src // 2, HIDDEN, :].astype(jnp.float32)
            for t in range(8):
                x, z_tile = where[t]
                row = hidden_ref[src, pl.ds(x * 4 + z_tile * 2 + core, 1), :]
                for b in range(4):
                    bias_ref[src, t, b] = jnp.broadcast_to(row[:, b : b + 1], (8, HEAD_DIM))

    queries = jnp.concatenate(
        [mine_ref[x, QUERIES, :] for x in range(4)] + [tile[...] for tile in far], 0
    )
    top = jnp.full((ROWS, 1), -3e30, jnp.float32)
    total = jnp.zeros((ROWS, 2 * HEAD_DIM), jnp.float32)
    for src in range(8):
        cache = caches[src % 2]
        scores = matmul(queries, cache[src // 2, KEYS, :], NT)
        scores = jnp.concatenate(
            [
                jnp.concatenate(
                    [
                        (
                            scores[t * Q_ROWS : (t + 1) * Q_ROWS, b * BLOCK : (b + 1) * BLOCK].reshape(
                                8, 8, BLOCK
                            )
                            + bias_ref[src, t, b][None]
                        ).reshape(Q_ROWS, BLOCK)
                        for b in range(4)
                    ],
                    1,
                )
                for t in range(8)
            ],
            0,
        )
        top, total = fold(scores, cache[src // 2, VALUES, :], top, total)

    for t in range(8):
        rows = slice(t * Q_ROWS, (t + 1) * Q_ROWS)
        tile_top, tile_total = top[rows], total[rows]
        x, z_tile = where[t]
        if t < 4:
            scores = matmul(mine_ref[t, QUERIES, :], mine_ref[t, OWN_KEYS, :], NT)
            tile_top, tile_total = fold(scores, mine_ref[t, OWN_VALUES, :], tile_top, tile_total)
        den = tile_total[:, HEAD_DIM:]
        part = (tile_total[:, :HEAD_DIM] / den).astype(jnp.bfloat16)
        out_ref[pl.ds(z_tile * 16 + x * 4, 4)] = part.reshape(4, 16, HEAD_DIM)
        logs_ref[head, z_tile * 4 + x] = tile_top * LOG2_SCALE + jnp.log2(den)

    @pl.when(head == HEADS_X - 1)
    def _():
        lane = lax.broadcasted_iota(jnp.int32, (ROWS, HEAD_DIM), 1)
        logs = logs_ref[0].reshape(ROWS, HEAD_DIM)
        for j in range(1, HEADS_X):
            logs = jnp.where(lane == j, logs_ref[j].reshape(ROWS, HEAD_DIM), logs)
        log_ref[...] = jnp.transpose(logs)[:8]


def attend(place, far, mine, theirs):
    heads = HEADS_X
    tile = pl.BlockSpec((Q_ROWS, HEAD_DIM), lambda j: (0, j))
    cache = pl.BlockSpec((4, mine.shape[1], HEAD_DIM), lambda j: (0, 0, j))
    return pl.pallas_call(
        attend_kernel,
        grid=(heads,),
        in_specs=[SMEM] + [tile] * 4 + [cache] * 2,
        out_specs=[
            pl.BlockSpec((32, 16, HEAD_DIM), lambda j: (0, j, 0)),
            pl.BlockSpec((8, ROWS), lambda j: (0, 0)),
        ],
        out_shape=[
            jax.ShapeDtypeStruct((32, heads * 16, HEAD_DIM), jnp.bfloat16),
            jax.ShapeDtypeStruct((8, ROWS), jnp.float32),
        ],
        scratch_shapes=[
            pltpu.VMEM((heads, 8, Q_ROWS, HEAD_DIM), jnp.float32),
            pltpu.VMEM((8, 16, HEAD_DIM), jnp.float32),
            pltpu.VMEM((8, 8, 4, 8, HEAD_DIM), jnp.float32),
        ],
        compiler_params=PARAMS,
        cost_estimate=pl.CostEstimate(
            flops=heads * 4 * ROWS * 4096 * 128, bytes_accessed=heads * 2**21, transcendentals=heads * 2**21
        ),
    )(place, *far, mine, theirs)


def final_kernel(part_ref, log_ref, gain_ref, out_ref, joined):
    split = jnp.sum(log_ref[...].astype(jnp.float32), axis=1)
    logs = [split[:16], split[16:]]
    top = jnp.maximum(*logs)
    shares = [jnp.exp2(a - top) for a in logs]
    whole = 1.0 / (shares[0] + shares[1])
    shares = [jnp.transpose(a * whole) for a in shares]
    squares = jnp.zeros((16, HEAD_DIM), jnp.float32)
    for x in range(4):
        for y in range(4):
            src = x * 4 + y
            value = (
                shares[0][:48, src : src + 1] * part_ref[src].astype(jnp.float32)
                + shares[1][:48, src : src + 1] * part_ref[16 + src].astype(jnp.float32)
            )
            value = value.astype(jnp.bfloat16).astype(jnp.float32)
            for head in range(HEADS_X):
                place = (y * 12 + x * HEADS_X + head) * HEAD_DIM
                piece = value[head * 16 : (head + 1) * 16]
                joined[:, place : place + HEAD_DIM] = piece
                squares = squares + piece * piece
    mean = jnp.sum(squares, axis=1, keepdims=True) * (1.0 / 6144)
    out_ref[...] = (
        joined[...] * lax.rsqrt(mean + 1e-06) * gain_ref[...].astype(jnp.float32)
    ).astype(jnp.bfloat16)


def thirds(logs):
    high = lax.reduce_precision(logs, 8, 7)
    middle = lax.reduce_precision(logs - high, 8, 7)
    low = lax.reduce_precision(logs - high - middle, 8, 7)
    rows = jnp.stack([high, middle, low], 1).astype(jnp.bfloat16)
    return jnp.pad(rows, ((0, 0), (0, STATS - 3), (0, HEAD_DIM - logs.shape[1])))


def local(queries, group_keys, group_values, cache_keys, cache_values, block_mask, gain):
    me = lax.axis_index("x")
    core = lax.axis_index("core")
    width = HEADS_X * HEAD_DIM

    mine = pack(cache_keys, cache_values, block_mask, group_keys, group_values, queries)
    mine = lax.all_to_all(mine, "x", 0, 0, tiled=True)

    def send(turn):
        block = lax.dynamic_slice_in_dim(queries, ((me + turn) % 4) * width, width, 1)
        route = [(x * 2 + z, (x + turn) % 4 * 2 + 1 - z) for x in range(4) for z in range(2)]
        return lax.ppermute(block, ("x", "z"), route)

    far = [send(turn) for turn in range(4)]
    mine, far = lax.optimization_barrier((mine, far))
    theirs = lax.ppermute(mine, "core", [(0, 1), (1, 0)])
    place = jnp.stack([(me - turn) % 4 for turn in range(4)] + [core, lax.axis_index("z")])
    part, logs = attend(place.astype(jnp.int32), far, mine, theirs)
    logs = logs[:HEADS_X]
    logs = logs.reshape(HEADS_X, 32, 16).transpose(1, 0, 2).reshape(32, 48)
    block = jnp.concatenate([part, thirds(logs)], 1)
    block = lax.all_to_all(block, ("z", "x", "head"), 0, 0, tiled=True)

    return pl.pallas_call(
        final_kernel,
        in_specs=[VMEM] * 3,
        out_specs=VMEM,
        out_shape=jax.ShapeDtypeStruct((16, 48 * HEAD_DIM), jnp.bfloat16),
        scratch_shapes=[pltpu.VMEM((16, 48 * HEAD_DIM), jnp.float32)],
        compiler_params=PARAMS,
    )(block[:, :48], block[:, 48:], gain.reshape(1, 48 * HEAD_DIM))


def solution(mesh):
    fine = Mesh(mesh.devices.reshape(8, 4, 2, 2, 4), ("video", "x", "z", "core", "head"))
    rows = ("video", "x", "z", "core")
    return jax.shard_map(
        local,
        mesh=fine,
        in_specs=(P(rows, "head"),) * 5 + (P("video", ("x", "z", "core")), P()),
        out_specs=P((*rows, "head"), None),
        check_vma=False,
    )
```

time: 694 us -> 140 us (0.20)
  starting transfers between devices: 342 us -> 57 us
  waiting for transfers between devices: 198 us -> 55 us
  local copies, waits for them, and re-layouts: 81.9 us -> 5.08 us
  other arithmetic: 43.2 us -> 1.95 us
  matrix products: 23.4 us -> 0 us
  Pallas kernels: 0 us -> 20 us
    ppermute x64 -> x5, starting transfers between devices: 329 us -> 37.6 us  [the longest x4 35.6 us: send(): return lax.ppermute(block, ('x', 'z'), route)]
    ppermute x64 -> x5, waiting for transfers between devices: 191 us -> 21 us  [the longest x4 14.8 us: send(): return lax.ppermute(block, ('x', 'z'), route)]
    reshape x32 -> x4, local copies, waits for them, and re-layouts: 42.4 us -> 0.83 us  [the longest x1 0.61 us: local(): gain.reshape(1, 48 * HEAD_DIM)]
    all_to_all x1 -> x2, waiting for transfers between devices: 6.32 us -> 34 us  [the longest x1 34 us: local(): block = lax.all_to_all(block, ('z', 'x', 'head'), 0, 0, tiled=True)]
    dot_general x34 -> x0, matrix products: 23.4 us -> none  [the longest x17 13.1 us: block_update(): jnp.einsum('qhd,khd->hqk', query_rows, keys, preferred_element_type=jnp.f...]
    add x16 -> x0, other arithmetic: 20.9 us -> none  [block_update(): denominator = denominator * factor + jnp.sum(weights, axis=-1)]
    pallas_call x0 -> x3, Pallas kernels: none -> 20 us  [the longest x1 13.3 us: attend(): pl.pallas_call(attend_kernel, grid=(heads,), in_specs=[SMEM] + [tile] * 4...]
    while x52 -> x0, local copies, waits for them, and re-layouts: 15.8 us -> none
  transfers between devices with their start and end apart: 65 -> 7, of which waited for: 23 -> 4; matrix products, arithmetic and copies ran while one was open for 17% -> 1% of each run, Pallas kernels for 0% -> 0%
where the time goes in v1:
time: 140 us; the launch traced here: 139 us
  starting transfers between devices  57 us (41%)
  waiting for transfers between devices  55 us (39%)
  Pallas kernels  20 us (14%)
  local copies, waits for them, and re-layouts  5.08 us (4%)
  other arithmetic  1.95 us (1%)
    ppermute x4, starting transfers between devices, send(): return lax.ppermute(block, ('x', 'z'), route)  35.6 us
    all_to_all x1, waiting for transfers between devices, local(): block = lax.all_to_all(block, ('z', 'x', 'head'), 0, 0, tiled=True)  34 us
    ppermute x4, waiting for transfers between devices, send(): return lax.ppermute(block, ('x', 'z'), route)  14.8 us
    all_to_all x1, starting transfers between devices, local(): block = lax.all_to_all(block, ('z', 'x', 'head'), 0, 0, tiled=True)  14.6 us
    pallas_call x1, Pallas kernels, attend(): pl.pallas_call(attend_kernel, grid=(heads,), in_specs=[SMEM] + [tile] * 4...  13.3 us
    ppermute x1, waiting for transfers between devices, local(): theirs = lax.ppermute(mine, 'core', [(0, 1), (1, 0)])  6.21 us
    all_to_all x1, starting transfers between devices, local(): mine = lax.all_to_all(mine, 'x', 0, 0, tiled=True)  4.9 us
    pallas_call x1, Pallas kernels, pack(): pl.pallas_call(pack_kernel, grid=(4,), in_specs=[big, big, pl.BlockSpec((...  4.44 us
  transfers between devices with their start and end apart: 7, of which 4 were waited for; matrix products, arithmetic and copies ran while one was open for 1% of the time, Pallas kernels for 0%

profile of v1, /device:TPU:32, one launch (start us, length us, event | category | flops | bytes accessed | tf_op | source)
XLA Modules:
  0.0 139.4 jit_solution(12665763460243743019)
XLA Ops:
  0.0 1.4 copy.14.mask_ref
  1.4 4.4 %shard_map.73 = bf16[4,1232,384]{2,1,0:T(8,128)(2,1)} custom-call(bf16[512,1536]{1,0:T(8,128)(2,1)} %k_ref.1, bf16[512,1536]{1,0:T(8,128)(2,1)} %v_ref.1, s32[16,4]{1,0:T(8,128)} %copy.14.mask_ref, bf16[64,1536]{1,0:T(8,128)(2,1)} %own_k_ref.1, bf16[64,1536]{1,0:T(8,128)(2,1)} %own_v_ref.1, bf16[64,1536]{1,0:T(8,128)(2,1)} %q_ref.1), custom_call_target="tpu_custom_call" | custom-call | tf_op jit(solution)/shard_map/pallas_call | solution.py:62
  5.8 0.0 copy-start
  5.8 4.9 %all-to-all-start = ((bf16[4,1232,384]{2,1,0:T(8,128)(2,1)}), bf16[4,1232,384]{2,1,0:T(8,128)(2,1)}, u32[]{:S(2)}, u32[]{:S(2)}) async-start(bf16[4,1232,384]{2,1,0:T(8,128)(2,1)} %shard_map.73), calls=%async_computation | async-start | bytes 7569408 | tf_op jit(solution)/shard_map/all_to_all | solution.py:207
  10.8 0.0 copy-done
  10.8 14.8 %collective-permute-start = (bf16[64,384]{1,0:T(8,128)(2,1)S(1)}, bf16[64,384]{1,0:T(8,128)(2,1)S(1)}, u32[]{:S(2)}, u32[]{:S(2)}) collective-permute-start(bf16[64,384]{1,0:T(8,128)(2,1)S(1)} %get-tuple-element.21), channel_id=1, source_target_pairs={{0,8},{8,0},{16,24},{24,16},{32,40},{40,32},{48,56},{56,48},{1,9},... | collective-permute-start | bytes 147464 | tf_op jit(solution)/shard_map/ppermute | solution.py:212
  25.6 3.2 %collective-permute-start.1 = (bf16[64,384]{1,0:T(8,128)(2,1)S(1)}, bf16[64,384]{1,0:T(8,128)(2,1)S(1)}, u32[]{:S(2)}, u32[]{:S(2)}) collective-permute-start(bf16[64,384]{1,0:T(8,128)(2,1)S(1)} %get-tuple-element.20), channel_id=1, source_target_pairs={{0,24},{8,16},{16,40},{24,32},{32,56},{40,48},{48,8},{56,0},{1,25}... | collective-permute-start | bytes 147464 | tf_op jit(solution)/shard_map/ppermute | solution.py:212
  28.9 14.8 %collective-permute-start.2 = (bf16[64,384]{1,0:T(8,128)(2,1)S(1)}, bf16[64,384]{1,0:T(8,128)(2,1)S(1)}, u32[]{:S(2)}, u32[]{:S(2)}) collective-permute-start(bf16[64,384]{1,0:T(8,128)(2,1)S(1)} %get-tuple-element.22), channel_id=1, source_target_pairs={{0,40},{8,32},{16,56},{24,48},{32,8},{40,0},{48,24},{56,16},{1,41}... | collective-permute-start | bytes 147464 | tf_op jit(solution)/shard_map/ppermute | solution.py:212
  43.7 2.8 %collective-permute-start.3 = (bf16[64,384]{1,0:T(8,128)(2,1)S(1)}, bf16[64,384]{1,0:T(8,128)(2,1)S(1)}, u32[]{:S(2)}, u32[]{:S(2)}) collective-permute-start(bf16[64,384]{1,0:T(8,128)(2,1)S(1)} %get-tuple-element.19), channel_id=1, source_target_pairs={{0,56},{8,48},{16,8},{24,0},{32,24},{40,16},{48,40},{56,32},{1,57}... | collective-permute-start | bytes 147464 | tf_op jit(solution)/shard_map/ppermute | solution.py:212
  46.5 0.0 collective-permute-done.refs_0_
  46.5 0.0 copy-start.2
  46.5 0.0 collective-permute-done.1.refs_1_
  46.5 0.0 copy-start.3
  46.5 2.7 %collective-permute-done.2.refs_2_ = bf16[64,384]{1,0:T(8,128)(2,1)S(1)} collective-permute-done((bf16[64,384]{1,0:T(8,128)(2,1)S(1)}, bf16[64,384]{1,0:T(8,128)(2,1)S(1)}, u32[]{:S(2)}, u32[]{:S(2)}) %collective-permute-start.2) | collective-permute-done | bytes 49184 | tf_op jit(solution)/shard_map/ppermute | solution.py:212
  49.2 0.0 copy-start.4
  49.2 12.2 %collective-permute-done.3.refs_3_ = bf16[64,384]{1,0:T(8,128)(2,1)S(1)} collective-permute-done((bf16[64,384]{1,0:T(8,128)(2,1)S(1)}, bf16[64,384]{1,0:T(8,128)(2,1)S(1)}, u32[]{:S(2)}, u32[]{:S(2)}) %collective-permute-start.3) | collective-permute-done | bytes 49184 | tf_op jit(solution)/shard_map/ppermute | solution.py:212
  61.3 0.0 copy-start.5
  61.3 0.0 all-to-all-done.refs_4_
  61.4 1.9 %collective-permute-start.4 = (bf16[4,1232,384]{2,1,0:T(8,128)(2,1)}, bf16[4,1232,384]{2,1,0:T(8,128)(2,1)}, u32[]{:S(2)}, u32[]{:S(2)}) collective-permute-start(bf16[4,1232,384]{2,1,0:T(8,128)(2,1)} %all-to-all-done.refs_4_), channel_id=1, source_target_pairs={{0,4},{4,0},{1,5},{5,1},{2,6},{6,2},{3,7},{7,3},{8,12},{12,8},{9,1... | collective-permute-start | bytes 11354120 | tf_op jit(solution)/shard_map/ppermute | solution.py:216
  63.3 0.6 stack.34.place_ref
  63.9 0.0 copy-start.1
  63.9 6.2 %collective-permute-done.4.refs_5_ = bf16[4,1232,384]{2,1,0:T(8,128)(2,1)} collective-permute-done((bf16[4,1232,384]{2,1,0:T(8,128)(2,1)}, bf16[4,1232,384]{2,1,0:T(8,128)(2,1)}, u32[]{:S(2)}, u32[]{:S(2)}) %collective-permute-start.4) | collective-permute-done | bytes 3784736 | tf_op jit(solution)/shard_map/ppermute | solution.py:216
  70.2 0.0 copy-done.2
  70.2 0.0 copy-done.3
  70.2 0.0 copy-done.4
  70.2 0.0 copy-done.5
  70.2 13.3 %shard_map.74 = (bf16[32,48,128]{2,1,0:T(8,128)(2,1)}, f32[8,512]{1,0:T(8,128)}) custom-call(s32[6]{0:T(128)} %stack.34.place_ref, bf16[64,384]{1,0:T(8,128)(2,1)} %copy-done.2, bf16[64,384]{1,0:T(8,128)(2,1)} %copy-done.3, bf16[64,384]{1,0:T(8,128)(2,1)} %copy-done.4, bf16[64,384]{1,0:T(8,128)(2,1)} %copy-done.5, ...), custom_call_target="tpu_custom_call" | custom-call | flops 3221225472 | bytes 6291456 | tf_op jit(solution)/shard_map/pallas_call | solution.py:142
  83.5 0.7 slice.9
  84.2 0.1 reshape.48
  84.3 0.1 copy.15
  84.3 0.1 copy.16
  84.4 0.1 copy.17
  84.6 0.1 fusion.8
  84.7 1.8 %pad_maximum_fusion = bf16[32,56,128]{2,1,0:T(8,128)(2,1)} fusion(bf16[32,8,128]{2,1,0:T(8,128)(2,1)S(1)} %fusion.8, bf16[32,48,128]{2,1,0:T(8,128)(2,1)} %get-tuple-element.17), kind=kLoop, calls=%fused_computation | loop fusion | flops 917504 | bytes 917504 | tf_op jit(solution)/shard_map/concatenate | solution.py:221
  86.5 14.6 %all-to-all-start.1 = ((bf16[32,56,128]{2,1,0:T(8,128)(2,1)}), bf16[32,56,128]{2,1,0:T(8,128)(2,1)S(1)}, u32[]{:S(2)}, u32[]{:S(2)}) async-start(bf16[32,56,128]{2,1,0:T(8,128)(2,1)} %pad_maximum_fusion), calls=%async_computation.1 | async-start | bytes 917504 | tf_op jit(solution)/shard_map/all_to_all | solution.py:222
  101.1 0.0 copy-done.1
  101.1 0.6 reshape.50.gain_ref
  101.7 34.0 %all-to-all-done.1 = bf16[32,56,128]{2,1,0:T(8,128)(2,1)S(1)} async-done(((bf16[32,56,128]{2,1,0:T(8,128)(2,1)}), bf16[32,56,128]{2,1,0:T(8,128)(2,1)S(1)}, u32[]{:S(2)}, u32[]{:S(2)}) %all-to-all-start.1) | async-done | bytes 458784 | tf_op jit(solution)/shard_map/all_to_all | solution.py:222
  135.7 0.8 slice.12.part_ref
  136.5 0.6 slice.13.log_ref
  137.1 2.3 %shard_map.75 = bf16[16,6144]{1,0:T(8,128)(2,1)} custom-call(bf16[32,48,128]{2,1,0:T(8,128)(2,1)} %slice.12.part_ref, bf16[32,8,128]{2,1,0:T(8,128)(2,1)} %slice.13.log_ref, bf16[1,6144]{1,0:T(2,128)(2,1)} %reshape.50.gain_ref), custom_call_target="tpu_custom_call" | custom-call | tf_op jit(solution)/shard_map/pallas_call | solution.py:224
  (4 shorter events, 0.1 us)
Async XLA Ops:
  5.8 5.0 %copy-start = (bf16[64,1536]{1,0:T(8,128)(2,1)S(1)}, bf16[64,1536]{1,0:T(8,128)(2,1)}, u32[]{:S(2)}) copy-start(bf16[64,1536]{1,0:T(8,128)(2,1)} %q_ref.1) | copy-start | bytes 589828
  5.8 55.6 %all-to-all-start = ((bf16[4,1232,384]{2,1,0:T(8,128)(2,1)}), bf16[4,1232,384]{2,1,0:T(8,128)(2,1)}, u32[]{:S(2)}, u32[]{:S(2)}) async-start(bf16[4,1232,384]{2,1,0:T(8,128)(2,1)} %shard_map.73), calls=%async_computation | async-start | bytes 7569408 | tf_op jit(solution)/shard_map/all_to_all | solution.py:207
  10.8 35.7 %collective-permute-start = (bf16[64,384]{1,0:T(8,128)(2,1)S(1)}, bf16[64,384]{1,0:T(8,128)(2,1)S(1)}, u32[]{:S(2)}, u32[]{:S(2)}) collective-permute-start(bf16[64,384]{1,0:T(8,128)(2,1)S(1)} %get-tuple-element.21), channel_id=1, source_target_pairs={{0,8},{8,0},{16,24},{24,16},{32,40},{40,32},{48,56},{56,48},{1,9},... | collective-permute-start | bytes 147464 | tf_op jit(solution)/shard_map/ppermute | solution.py:212
  25.6 20.9 %collective-permute-start.1 = (bf16[64,384]{1,0:T(8,128)(2,1)S(1)}, bf16[64,384]{1,0:T(8,128)(2,1)S(1)}, u32[]{:S(2)}, u32[]{:S(2)}) collective-permute-start(bf16[64,384]{1,0:T(8,128)(2,1)S(1)} %get-tuple-element.20), channel_id=1, source_target_pairs={{0,24},{8,16},{16,40},{24,32},{32,56},{40,48},{48,8},{56,0},{1,25}... | collective-permute-start | bytes 147464 | tf_op jit(solution)/shard_map/ppermute | solution.py:212
  28.9 20.3 %collective-permute-start.2 = (bf16[64,384]{1,0:T(8,128)(2,1)S(1)}, bf16[64,384]{1,0:T(8,128)(2,1)S(1)}, u32[]{:S(2)}, u32[]{:S(2)}) collective-permute-start(bf16[64,384]{1,0:T(8,128)(2,1)S(1)} %get-tuple-element.22), channel_id=1, source_target_pairs={{0,40},{8,32},{16,56},{24,48},{32,8},{40,0},{48,24},{56,16},{1,41}... | collective-permute-start | bytes 147464 | tf_op jit(solution)/shard_map/ppermute | solution.py:212
  43.7 17.7 %collective-permute-start.3 = (bf16[64,384]{1,0:T(8,128)(2,1)S(1)}, bf16[64,384]{1,0:T(8,128)(2,1)S(1)}, u32[]{:S(2)}, u32[]{:S(2)}) collective-permute-start(bf16[64,384]{1,0:T(8,128)(2,1)S(1)} %get-tuple-element.19), channel_id=1, source_target_pairs={{0,56},{8,48},{16,8},{24,0},{32,24},{40,16},{48,40},{56,32},{1,57}... | collective-permute-start | bytes 147464 | tf_op jit(solution)/shard_map/ppermute | solution.py:212
  46.5 23.7 %copy-start.2 = (bf16[64,384]{1,0:T(8,128)(2,1)}, bf16[64,384]{1,0:T(8,128)(2,1)S(1)}, u32[]{:S(2)}) copy-start(bf16[64,384]{1,0:T(8,128)(2,1)S(1)} %collective-permute-done.refs_0_) | copy-start | bytes 147460
  46.5 23.6 %copy-start.3 = (bf16[64,384]{1,0:T(8,128)(2,1)}, bf16[64,384]{1,0:T(8,128)(2,1)S(1)}, u32[]{:S(2)}) copy-start(bf16[64,384]{1,0:T(8,128)(2,1)S(1)} %collective-permute-done.1.refs_1_) | copy-start | bytes 147460
  49.2 21.0 %copy-start.4 = (bf16[64,384]{1,0:T(8,128)(2,1)}, bf16[64,384]{1,0:T(8,128)(2,1)S(1)}, u32[]{:S(2)}) copy-start(bf16[64,384]{1,0:T(8,128)(2,1)S(1)} %collective-permute-done.2.refs_2_) | copy-start | bytes 147460
  61.3 8.8 %copy-start.5 = (bf16[64,384]{1,0:T(8,128)(2,1)}, bf16[64,384]{1,0:T(8,128)(2,1)S(1)}, u32[]{:S(2)}) copy-start(bf16[64,384]{1,0:T(8,128)(2,1)S(1)} %collective-permute-done.3.refs_3_) | copy-start | bytes 147460
  61.4 8.8 %collective-permute-start.4 = (bf16[4,1232,384]{2,1,0:T(8,128)(2,1)}, bf16[4,1232,384]{2,1,0:T(8,128)(2,1)}, u32[]{:S(2)}, u32[]{:S(2)}) collective-permute-start(bf16[4,1232,384]{2,1,0:T(8,128)(2,1)} %all-to-all-done.refs_4_), channel_id=1, source_target_pairs={{0,4},{4,0},{1,5},{5,1},{2,6},{6,2},{3,7},{7,3},{8,12},{12,8},{9,1... | collective-permute-start | bytes 11354120 | tf_op jit(solution)/shard_map/ppermute | solution.py:216
  63.9 37.1 %copy-start.1 = (bf16[6144]{0:T(1024)(128)(2,1)S(1)}, bf16[6144]{0:T(1024)(128)(2,1)}, u32[]{:S(2)}) copy-start(bf16[6144]{0:T(1024)(128)(2,1)} %param.13) | copy-start | bytes 36868
  86.5 49.2 %all-to-all-start.1 = ((bf16[32,56,128]{2,1,0:T(8,128)(2,1)}), bf16[32,56,128]{2,1,0:T(8,128)(2,1)S(1)}, u32[]{:S(2)}, u32[]{:S(2)}) async-start(bf16[32,56,128]{2,1,0:T(8,128)(2,1)} %pad_maximum_fusion), calls=%async_computation.1 | async-start | bytes 917504 | tf_op jit(solution)/shard_map/all_to_all | solution.py:222

commit v2 on v1

v2 whole, which is shorter than its diff:
```python
import jax
import jax.numpy as jnp
from jax import lax
from jax.experimental import pallas as pl
from jax.experimental.pallas import tpu as pltpu
from jax.sharding import Mesh
from jax.sharding import PartitionSpec as P

HEAD_DIM = 128
BLOCK = 128
HEADS_X = 3
Q_ROWS = 64
ROWS = 8 * Q_ROWS
TOK = 512
LOG2_SCALE = HEAD_DIM ** (-0.5) * 1.4426950408889634
NEG = -1e30
KEYS = slice(0, TOK)
VALUES = slice(TOK, 2 * TOK)
QUERIES = slice(2 * TOK, 2 * TOK + Q_ROWS)
HIDDEN = slice(2 * TOK + Q_ROWS, 2 * TOK + Q_ROWS + 16)
PACKET = 2 * TOK + Q_ROWS + 16
LOGS = slice(HEADS_X * Q_ROWS, HEADS_X * Q_ROWS + 16)
FAR = HEADS_X * Q_ROWS + 16
NT = (((1,), (1,)), ((), ()))
NN = (((1,), (0,)), ((), ()))
VMEM = pl.BlockSpec(memory_space=pltpu.VMEM)
SMEM = pl.BlockSpec(memory_space=pltpu.SMEM)
PARAMS = pltpu.CompilerParams(vmem_limit_bytes=40 * 2**20)


def with_ones(values):
    return jnp.concatenate([values, jnp.ones((values.shape[0], HEAD_DIM), jnp.bfloat16)], 1)


def matmul(a, b, dims):
    return lax.dot_general(a, b, dims, preferred_element_type=jnp.float32)


def fold(scores, values, top, total):
    new_top = jnp.maximum(top, jnp.max(scores, axis=1, keepdims=True))
    weights = jnp.exp2((scores - new_top) * LOG2_SCALE).astype(jnp.bfloat16)
    factor = jnp.exp2((top - new_top) * LOG2_SCALE)
    return new_top, total * factor + matmul(weights, with_ones(values), NN)


def pack_kernel(place_ref, k_ref, v_ref, mask_ref, q_ref, own_k_ref, own_v_ref, out_ref, *turn_refs):
    hidden = jnp.where(mask_ref[...] > 0, 0.0, NEG)
    hidden = jnp.concatenate([hidden, hidden], 0)
    hidden = jnp.concatenate([hidden, jnp.zeros((8, HEAD_DIM - 16), jnp.float32)], 1)
    hidden = jnp.transpose(hidden)[:16]
    hidden = jnp.concatenate([hidden, jnp.zeros((16, HEAD_DIM - 8), jnp.float32)], 1)
    out_ref[0, KEYS, :] = k_ref[...]
    out_ref[0, VALUES, :] = v_ref[...]
    out_ref[0, HIDDEN, :] = jnp.concatenate([hidden.astype(jnp.bfloat16)] * HEADS_X, 1)
    out_ref[0, QUERIES, :] = q_ref[...]
    for turn in range(4):

        @pl.when(pl.program_id(0) == place_ref[6 + turn])
        def _(turn=turn):
            rows = slice(turn % 2 * Q_ROWS, (turn % 2 + 1) * Q_ROWS)
            turn_refs[turn // 2][rows, :] = q_ref[...]
            turn_refs[2 + turn][:Q_ROWS, :] = own_k_ref[...]
            turn_refs[2 + turn][Q_ROWS:, :] = own_v_ref[...]


def pack(place, keys, values, mask, queries, own_keys, own_values):
    width = HEADS_X * HEAD_DIM
    big = pl.BlockSpec((TOK, width), lambda x: (0, x))
    small = pl.BlockSpec((Q_ROWS, width), lambda x: (0, x))
    sizes = [(2 * Q_ROWS, width)] * 6
    packet, *turns = pl.pallas_call(
        pack_kernel,
        grid=(4,),
        in_specs=[SMEM, big, big, pl.BlockSpec((4, 16), lambda x: (0, 0)), small, small, small],
        out_specs=[pl.BlockSpec((1, PACKET, width), lambda x: (x, 0, 0))]
        + [pl.BlockSpec(size, lambda x: (0, 0)) for size in sizes],
        out_shape=[jax.ShapeDtypeStruct((4, PACKET, width), jnp.bfloat16)]
        + [jax.ShapeDtypeStruct(size, jnp.bfloat16) for size in sizes],
        compiler_params=pltpu.CompilerParams(vmem_limit_bytes=62 * 2**20),
    )(place, keys, values, mask.T, queries, own_keys, own_values)
    return packet, turns[:2], turns[2:]


def put_hidden(cache_ref, hidden_ref):
    for src in range(4):
        hidden = cache_ref[src, HIDDEN, :].astype(jnp.float32)
        for b in range(4):
            hidden_ref[src, b] = jnp.broadcast_to(hidden[:, b : b + 1], (16, HEAD_DIM))


def over_cache(queries, rows, cache_ref, hidden_ref, top, total):
    product = matmul(queries, cache_ref[0, KEYS, :], NT)
    for src in range(4):
        scores = jnp.concatenate(
            [
                jnp.concatenate(
                    [
                        product[t * Q_ROWS : (t + 1) * Q_ROWS, b * BLOCK : (b + 1) * BLOCK]
                        + jnp.broadcast_to(hidden_ref[src, b, pl.ds(row, 1), :], (Q_ROWS, BLOCK))
                        for b in range(4)
                    ],
                    1,
                )
                for t, row in enumerate(rows)
            ],
            0,
        )
        if src < 3:
            product = matmul(queries, cache_ref[src + 1, KEYS, :], NT)
        top, total = fold(scores, cache_ref[src, VALUES, :], top, total)
    return top, total


def far_rows(place_ref):
    return [place_ref[t] * 4 + (1 - place_ref[5]) * 2 + place_ref[4] for t in range(4)]


def first_kernel(place_ref, f0, f1, f2, f3, mine_ref, top_ref, total_ref, hidden_ref):
    @pl.when(pl.program_id(0) == 0)
    def _():
        put_hidden(mine_ref, hidden_ref)

    queries = jnp.concatenate([tile[...] for tile in (f0, f1, f2, f3)], 0)
    top = jnp.full((4 * Q_ROWS, 1), -3e30, jnp.float32)
    total = jnp.zeros((4 * Q_ROWS, 2 * HEAD_DIM), jnp.float32)
    top, total = over_cache(queries, far_rows(place_ref), mine_ref, hidden_ref, top, total)
    top_ref[0] = jnp.broadcast_to(top, (4 * Q_ROWS, HEAD_DIM))
    total_ref[0] = total


def far_kernel(
    place_ref, f0, f1, f2, f3, theirs_ref, top_ref, total_ref, out_ref, logs_ref, hidden_ref
):
    head = pl.program_id(0)

    @pl.when(head == 0)
    def _():
        put_hidden(theirs_ref, hidden_ref)

    queries = jnp.concatenate([tile[...] for tile in (f0, f1, f2, f3)], 0)
    top = jnp.max(top_ref[0], axis=1, keepdims=True)
    top, total = over_cache(queries, far_rows(place_ref), theirs_ref, hidden_ref, top, total_ref[0])
    den = total[:, HEAD_DIM:]
    part = total[:, :HEAD_DIM] / den
    logs = top * LOG2_SCALE + jnp.log2(den)
    part = part.astype(jnp.bfloat16)
    for t in range(4):
        rows = slice(t * Q_ROWS, (t + 1) * Q_ROWS)
        out_ref[place_ref[t], pl.ds(pl.multiple_of(head * Q_ROWS, Q_ROWS), Q_ROWS), :] = part[rows]
        logs_ref[head, place_ref[t]] = logs[rows]

    @pl.when(head == HEADS_X - 1)
    def _():
        lane = lax.broadcasted_iota(jnp.int32, (Q_ROWS, HEAD_DIM), 1)
        for x in range(4):
            logs = jnp.zeros((Q_ROWS, HEAD_DIM), jnp.float32)
            for j in range(HEADS_X):
                logs = jnp.where(lane == j, logs_ref[j, x], logs)
            logs = jnp.transpose(logs)[:8]
            high = logs.astype(jnp.bfloat16).astype(jnp.float32)
            middle = (logs - high).astype(jnp.bfloat16).astype(jnp.float32)
            low = logs - high - middle
            rows = jnp.concatenate([high[:4], middle[:4], low], 0)
            rows = jnp.concatenate([rows, jnp.zeros((16, HEAD_DIM - Q_ROWS), jnp.float32)], 1)
            out_ref[x, LOGS, :] = rows.astype(jnp.bfloat16)


def near_kernel(place_ref, mine_ref, theirs_ref, top_ref, total_ref, hidden_ref):
    @pl.when(pl.program_id(0) == 0)
    def _():
        put_hidden(mine_ref, hidden_ref.at[0])
        put_hidden(theirs_ref, hidden_ref.at[1])

    mask_rows = [t * 4 + place_ref[5] * 2 + place_ref[4] for t in range(4)]
    queries = jnp.concatenate([mine_ref[x, QUERIES, :] for x in range(4)], 0)
    top = jnp.full((4 * Q_ROWS, 1), -3e30, jnp.float32)
    total = jnp.zeros((4 * Q_ROWS, 2 * HEAD_DIM), jnp.float32)
    top, total = over_cache(queries, mask_rows, mine_ref, hidden_ref.at[0], top, total)
    top, total = over_cache(queries, mask_rows, theirs_ref, hidden_ref.at[1], top, total)
    top_ref[0] = jnp.broadcast_to(top, (4 * Q_ROWS, HEAD_DIM)).reshape(4, Q_ROWS, HEAD_DIM)
    total_ref[0] = total.reshape(4, Q_ROWS, 2 * HEAD_DIM)


def own_kernel(place_ref, q_ref, o0, o1, o2, o3, top_ref, total_ref, out_ref, log_ref):
    for t, own_ref in enumerate((o0, o1, o2, o3)):
        x = place_ref[t]
        for j in range(HEADS_X):
            cols = slice(j * HEAD_DIM, (j + 1) * HEAD_DIM)
            scores = matmul(q_ref[x, :, cols], own_ref[:Q_ROWS, cols], NT)
            top = jnp.max(top_ref[j, x], axis=1, keepdims=True)
            top, total = fold(scores, own_ref[Q_ROWS:, cols], top, total_ref[j, x])
            den = total[:, HEAD_DIM:]
            out_ref[j, x] = total[:, :HEAD_DIM] / den
            log_ref[j, x] = top * LOG2_SCALE + jnp.log2(den)


def join_kernel(near_ref, near_log_ref, far_ref, out_ref):
    for x in range(4):
        logs = far_ref[x, LOGS, :].astype(jnp.float32)
        logs = logs[:4] + logs[4:8] + logs[8:12]
        logs = jnp.transpose(jnp.concatenate([logs, logs], 0))
        for j in range(HEADS_X):
            far_log = logs[:Q_ROWS, j : j + 1]
            near_log = near_log_ref[j, x]
            top = jnp.maximum(near_log, far_log)
            near_share, far_share = jnp.exp2(near_log - top), jnp.exp2(far_log - top)
            far = far_ref[x, j * Q_ROWS : (j + 1) * Q_ROWS, :].astype(jnp.float32)
            value = (near_ref[j, x] * near_share + far * far_share) / (near_share + far_share)
            value = value.astype(jnp.bfloat16)
            for y in range(4):
                out_ref[x * 4 + y, j * 16 : (j + 1) * 16, :] = value[y * 16 : (y + 1) * 16]


def norm_kernel(part_ref, gain_ref, out_ref):
    squares = jnp.zeros((16, HEAD_DIM), jnp.float32)
    for src in range(16):
        value = part_ref[src].astype(jnp.float32)
        value = value * value
        for j in range(HEADS_X):
            squares = squares + value[j * 16 : (j + 1) * 16]
    mean = jnp.sum(squares, axis=1, keepdims=True) * (1.0 / 6144)
    factor = lax.rsqrt(mean + 1e-06)
    for x in range(4):
        for y in range(4):
            for j in range(HEADS_X):
                value = part_ref[x * 4 + y, j * 16 : (j + 1) * 16, :].astype(jnp.float32)
                place = (y * 12 + x * HEADS_X + j) * HEAD_DIM
                cols = slice(place, place + HEAD_DIM)
                gain = gain_ref[:, cols].astype(jnp.float32)
                out_ref[:, cols] = (value * factor * gain).astype(jnp.bfloat16)


def attend(place, far, own, mine, theirs):
    heads = HEADS_X
    tiles = [pl.BlockSpec((Q_ROWS, HEAD_DIM), lambda j, row=row: (row, j)) for row in (0, 0, 0, 1)]
    cache = pl.BlockSpec((4, PACKET, HEAD_DIM), lambda j: (0, 0, j))

    state = [
        pl.BlockSpec((1, 4 * Q_ROWS, width), lambda j: (j, 0, 0)) for width in (HEAD_DIM, 2 * HEAD_DIM)
    ]
    state_shape = [
        jax.ShapeDtypeStruct((heads, 4 * Q_ROWS, width), jnp.float32) for width in (HEAD_DIM, 2 * HEAD_DIM)
    ]
    hidden = pltpu.VMEM((4, 4, 16, HEAD_DIM), jnp.float32)

    def common(keys):
        return dict(
            grid=(heads,),
            compiler_params=PARAMS,
            cost_estimate=pl.CostEstimate(
                flops=heads * 16 * Q_ROWS * keys * 128,
                bytes_accessed=heads * keys * 2**9,
                transcendentals=heads * 4 * Q_ROWS * keys,
            ),
        )

    top, total = pl.pallas_call(
        first_kernel,
        in_specs=[SMEM] + tiles + [cache],
        out_specs=state,
        out_shape=state_shape,
        scratch_shapes=[hidden],
        **common(2048),
    )(place, *far, mine)
    far_out = pl.pallas_call(
        far_kernel,
        in_specs=[SMEM] + tiles + [cache] + state,
        out_specs=pl.BlockSpec((4, FAR, HEAD_DIM), lambda j: (0, 0, 0)),
        out_shape=jax.ShapeDtypeStruct((4, FAR, HEAD_DIM), jnp.bfloat16),
        scratch_shapes=[pltpu.VMEM((heads, 4, Q_ROWS, HEAD_DIM), jnp.float32), hidden],
        **common(2048),
    )(place, *far, theirs, top, total)
    far_out, own = lax.optimization_barrier((far_out, own))
    far_out = lax.ppermute(far_out, "z", [(0, 1), (1, 0)])
    own = [own[0]] + [
        lax.ppermute(own[turn], "x", [(x, (x + turn) % 4) for x in range(4)]) for turn in range(1, 4)
    ]
    near = [
        pl.BlockSpec((1, 4, Q_ROWS, width), lambda j: (j, 0, 0, 0)) for width in (HEAD_DIM, 2 * HEAD_DIM)
    ]
    top, total = pl.pallas_call(
        near_kernel,
        in_specs=[SMEM, cache, cache],
        out_specs=near,
        out_shape=[
            jax.ShapeDtypeStruct((heads, 4, Q_ROWS, width), jnp.float32) for width in (HEAD_DIM, 2 * HEAD_DIM)
        ],
        scratch_shapes=[pltpu.VMEM((2, 4, 4, 16, HEAD_DIM), jnp.float32)],
        **common(4096),
    )(place, mine, theirs)

    def whole(shape):
        return pl.BlockSpec(shape, lambda i: (0,) * len(shape))

    near_shape = (heads, 4, Q_ROWS, HEAD_DIM)
    near_out, near_log = pl.pallas_call(
        own_kernel,
        grid=(1,),
        in_specs=[
            SMEM,
            pl.BlockSpec((4, Q_ROWS, heads * HEAD_DIM), lambda i: (0, QUERIES.start // Q_ROWS, 0)),
            *[whole((2 * Q_ROWS, heads * HEAD_DIM))] * 4,
            whole(top.shape),
            whole(total.shape),
        ],
        out_specs=[whole(near_shape)] * 2,
        out_shape=[jax.ShapeDtypeStruct(near_shape, jnp.float32)] * 2,
        compiler_params=PARAMS,
    )(place, mine, *own, top, total)
    return pl.pallas_call(
        join_kernel,
        in_specs=[VMEM] * 3,
        out_specs=VMEM,
        out_shape=jax.ShapeDtypeStruct((16, heads * 16, HEAD_DIM), jnp.bfloat16),
        compiler_params=PARAMS,
    )(near_out, near_log, far_out)


def local(queries, group_keys, group_values, cache_keys, cache_values, block_mask, gain):
    me, z, core = (lax.axis_index(axis) for axis in ("x", "z", "core"))
    place = [(me - turn) % 4 for turn in range(4)] + [core, z] + [(me + turn) % 4 for turn in range(4)]
    place = jnp.stack(place).astype(jnp.int32)

    packet, blocks, own = pack(
        place, cache_keys, cache_values, block_mask, queries, group_keys, group_values
    )
    mine = lax.all_to_all(packet, "x", 0, 0, tiled=True)

    def send(block, turn):
        route = [(x * 2 + z, (x + turn) % 4 * 2 + 1 - z) for x in range(4) for z in range(2)]
        return lax.ppermute(block, ("x", "z"), route)

    far = [send(blocks[0], 0), send(blocks[1], 2)]
    odd = jnp.concatenate([block[Q_ROWS:] for block in far], 0)
    odd = lax.ppermute(odd, "x", [(x, (x + 1) % 4) for x in range(4)])
    mine, far = lax.optimization_barrier((mine, [far[0], odd, far[1]]))
    far = [pltpu.with_memory_space_constraint(a, pltpu.HBM) for a in far]
    far.append(far[1])
    theirs = lax.ppermute(mine, "core", [(0, 1), (1, 0)])
    block = attend(place, far, own, mine, theirs)
    block = lax.all_to_all(block, ("x", "head"), 0, 0, tiled=True)
    return pl.pallas_call(
        norm_kernel,
        in_specs=[VMEM] * 2,
        out_specs=VMEM,
        out_shape=jax.ShapeDtypeStruct((16, 48 * HEAD_DIM), jnp.bfloat16),
        compiler_params=PARAMS,
    )(block, gain.reshape(1, 48 * HEAD_DIM))


def solution(mesh):
    fine = Mesh(mesh.devices.reshape(8, 4, 2, 2, 4), ("video", "x", "z", "core", "head"))
    rows = ("video", "x", "z", "core")
    return jax.shard_map(
        local,
        mesh=fine,
        in_specs=(P(rows, "head"),) * 5 + (P("video", ("x", "z", "core")), P()),
        out_specs=P((*rows, "head"), None),
        check_vma=False,
    )
```

time: 140 us -> 118 us (0.84)
  waiting for transfers between devices: 55 us -> 34 us
  local copies, waits for them, and re-layouts: 5.08 us -> 0.76 us
  Pallas kernels: 20 us -> 24.2 us
  other arithmetic: 1.95 us -> 0.01 us
    all_to_all x2, waiting for transfers between devices: 34 us -> 8.05 us  [the longest x1 8.04 us: local(): block = lax.all_to_all(block, ('x', 'head'), 0, 0, tiled=True)]
    ppermute x0 -> x5, starting transfers between devices: none -> 24.6 us  [the longest x1 13.2 us: attend(): far_out = lax.ppermute(far_out, 'z', [(0, 1), (1, 0)])]
    ppermute x4 -> x2, starting transfers between devices: 35.6 us -> 19.7 us  [send(): return lax.ppermute(block, ('x', 'z'), route)]
    all_to_all x2, starting transfers between devices: 19.5 us -> 11.3 us  [the longest x1 6.91 us: local(): block = lax.all_to_all(block, ('x', 'head'), 0, 0, tiled=True)]
    ppermute x0 -> x5, waiting for transfers between devices: none -> 5.23 us  [the longest x1 5.22 us: local(): odd = lax.ppermute(odd, 'x', [(x, (x + 1) % 4) for x in range(4)])]
    pallas_call x3 -> x7, Pallas kernels: 20 us -> 24.2 us  [the longest x1 6.44 us: attend(): pl.pallas_call(near_kernel, in_specs=[SMEM, cache, cache], out_specs=near...]
    ppermute x1, waiting for transfers between devices: 6.21 us -> 2.01 us  [local(): theirs = lax.ppermute(mine, 'core', [(0, 1), (1, 0)])]
    ppermute x4 -> x2, waiting for transfers between devices: 14.8 us -> 18.7 us  [send(): return lax.ppermute(block, ('x', 'z'), route)]
  transfers between devices with their start and end apart: 7 -> 10, of which waited for: 4 -> 5; matrix products, arithmetic and copies ran while one was open for 1% -> 0% of each run, Pallas kernels for 0% -> 12%
where the time goes in v2:
time: 118 us; the launch traced here: 117 us
  starting transfers between devices  57.6 us (49%)
  waiting for transfers between devices  34 us (29%)
  Pallas kernels  24.2 us (21%)
    ppermute x2, starting transfers between devices, send(): return lax.ppermute(block, ('x', 'z'), route)  19.7 us
    ppermute x2, waiting for transfers between devices, send(): return lax.ppermute(block, ('x', 'z'), route)  18.7 us
    ppermute x1, starting transfers between devices, attend(): far_out = lax.ppermute(far_out, 'z', [(0, 1), (1, 0)])  13.2 us
    ppermute x3, starting transfers between devices, attend(): lax.ppermute(own[turn], 'x', [(x, (x + turn) % 4) for x in range(4)])  8.97 us
    all_to_all x1, waiting for transfers between devices, local(): block = lax.all_to_all(block, ('x', 'head'), 0, 0, tiled=True)  8.04 us
    all_to_all x1, starting transfers between devices, local(): block = lax.all_to_all(block, ('x', 'head'), 0, 0, tiled=True)  6.91 us
    pallas_call x1, Pallas kernels, attend(): pl.pallas_call(near_kernel, in_specs=[SMEM, cache, cache], out_specs=near...  6.44 us
    ppermute x1, waiting for transfers between devices, local(): odd = lax.ppermute(odd, 'x', [(x, (x + 1) % 4) for x in range(4)])  5.22 us
  transfers between devices with their start and end apart: 10, of which 5 were waited for; matrix products, arithmetic and copies ran while one was open for 0% of the time, Pallas kernels for 12%

profile of v2, /device:TPU:32, one launch (start us, length us, event | category | flops | bytes accessed | tf_op | source)
XLA Modules:
  0.0 116.9 jit_solution(6879244447240894718)
XLA Ops:
  0.0 0.7 stack.40.place_ref
  0.7 4.7 %shard_map.73 = (bf16[4,1104,384]{2,1,0:T(8,128)(2,1)}, bf16[128,384]{1,0:T(8,128)(2,1)}, bf16[128,384]{1,0:T(8,128)(2,1)}, bf16[128,384]{1,0:T(8,128)(2,1)}, bf...) custom-call(s32[10]{0:T(128)} %stack.40.place_ref, bf16[512,1536]{1,0:T(8,128)(2,1)} %k_ref.1, ...), custom_call_target="tpu_custom_call" | custom-call | tf_op jit(solution)/shard_map/pallas_call | solution.py:71
  5.4 0.0 copy-start.9
  5.4 0.0 copy-start.1
  5.4 4.4 %all-to-all-start = ((bf16[4,1104,384]{2,1,0:T(8,128)(2,1)}), bf16[4,1104,384]{2,1,0:T(8,128)(2,1)S(1)}, u32[]{:S(2)}, u32[]{:S(2)}) async-start(bf16[4,1104,384]{2,1,0:T(8,128)(2,1)} %get-tuple-element.27), calls=%async_computation | async-start | bytes 6782976 | tf_op jit(solution)/shard_map/all_to_all | solution.py:327
  9.9 17.8 %collective-permute-start.1 = (bf16[128,384]{1,0:T(8,128)(2,1)}, bf16[128,384]{1,0:T(8,128)(2,1)S(1)}, u32[]{:S(2)}, u32[]{:S(2)}) collective-permute-start(bf16[128,384]{1,0:T(8,128)(2,1)} %get-tuple-element.29), channel_id=1, source_target_pairs={{0,40},{8,32},{16,56},{24,48},{32,8},{40,0},{48,24},{56,16},{1,41}... | collective-permute-start | bytes 294920 | tf_op jit(solution)/shard_map/ppermute | solution.py:331
  27.6 0.0 copy-done.9
  27.6 1.9 %collective-permute-start = (bf16[128,384]{1,0:T(8,128)(2,1)S(1)}, bf16[128,384]{1,0:T(8,128)(2,1)S(1)}, u32[]{:S(2)}, u32[]{:S(2)}) collective-permute-start(bf16[128,384]{1,0:T(8,128)(2,1)S(1)} %copy-done.9), channel_id=1, source_target_pairs={{0,8},{8,0},{16,24},{24,16},{32,40},{40,32},{48,56},{56,48},{1,9},... | collective-permute-start | bytes 294920 | tf_op jit(solution)/shard_map/ppermute | solution.py:331
  29.6 13.4 %collective-permute-done.1.f2 = bf16[128,384]{1,0:T(8,128)(2,1)S(1)} collective-permute-done((bf16[128,384]{1,0:T(8,128)(2,1)}, bf16[128,384]{1,0:T(8,128)(2,1)S(1)}, u32[]{:S(2)}, u32[]{:S(2)}) %collective-permute-start.1) | collective-permute-done | bytes 98336 | tf_op jit(solution)/shard_map/ppermute | solution.py:331
  43.0 0.0 copy-start.3
  43.0 5.3 %collective-permute-done.f0 = bf16[128,384]{1,0:T(8,128)(2,1)S(1)} collective-permute-done((bf16[128,384]{1,0:T(8,128)(2,1)S(1)}, bf16[128,384]{1,0:T(8,128)(2,1)S(1)}, u32[]{:S(2)}, u32[]{:S(2)}) %collective-permute-start) | collective-permute-done | bytes 98336 | tf_op jit(solution)/shard_map/ppermute | solution.py:331
  48.3 0.0 copy-start.4
  48.3 2.5 %collective-permute-start.2 = (bf16[128,384]{1,0:T(8,128)(2,1)S(1)}, bf16[128,384]{1,0:T(8,128)(2,1)S(1)}, u32[]{:S(2)}, u32[]{:S(2)}) collective-permute-start(bf16[128,384]{1,0:T(8,128)(2,1)S(1)} %pad_maximum_fusion), channel_id=1, source_target_pairs={{0,16},{16,32},{32,48},{48,0},{1,17},{17,33},{33,49},{49,1},{2,18}... | collective-permute-start | bytes 294920 | tf_op jit(solution)/shard_map/ppermute | solution.py:335
  50.8 0.0 copy-done.3
  50.8 0.0 copy-done.4
  50.8 5.2 %collective-permute-done.2.f1.f3 = bf16[128,384]{1,0:T(8,128)(2,1)S(1)} collective-permute-done((bf16[128,384]{1,0:T(8,128)(2,1)S(1)}, bf16[128,384]{1,0:T(8,128)(2,1)S(1)}, u32[]{:S(2)}, u32[]{:S(2)}) %collective-permute-start.2) | collective-permute-done | bytes 98336 | tf_op jit(solution)/shard_map/ppermute | solution.py:335
  56.0 0.0 copy-start.2
  56.0 0.0 all-to-all-done.mine_ref.q_ref
  56.0 1.9 %collective-permute-start.3 = (bf16[4,1104,384]{2,1,0:T(8,128)(2,1)S(1)}, bf16[4,1104,384]{2,1,0:T(8,128)(2,1)S(1)}, u32[]{:S(2)}, u32[]{:S(2)}) collective-permute-start(bf16[4,1104,384]{2,1,0:T(8,128)(2,1)S(1)} %all-to-all-done.mine_ref.q_ref), channel_id=1, source_target_pairs={{0,4},{4,0},{1,5},{5,1},{2,6},{6,2},{3,7},{7,3},{8,12},{12,8},{9,1... | collective-permute-start | bytes 10174472 | tf_op jit(solution)/shard_map/ppermute | solution.py:339
  57.9 0.0 copy-done.2
  58.0 0.0 copy-done.1
  58.0 3.9 %shard_map.74 = (f32[3,256,128]{2,1,0:T(8,128)S(1)}, f32[3,256,256]{2,1,0:T(8,128)S(1)}) custom-call(s32[10]{0:T(128)S(1)} %copy-done.1, bf16[128,384]{1,0:T(8,128)(2,1)} %copy-done.4, bf16[128,384]{1,0:T(8,128)(2,1)} %copy-done.2, bf16[128,384]{1,0:T(8,128)(2,1)} %copy-done.3, bf16[128,384]{1,0:T(8,128)(2,1)} %copy-done.2, ...), custom_call_target="tpu_custom_call" | custom-call | flops 805306368 | bytes 3145728 | tf_op jit(solution)/shard_map/pallas_call | solution.py:257
  61.9 0.0 copy-start.8
  61.9 0.0 copy-start.7
  61.9 0.0 copy-start.6
  61.9 2.0 %collective-permute-done.3.theirs_ref = bf16[4,1104,384]{2,1,0:T(8,128)(2,1)S(1)} collective-permute-done((bf16[4,1104,384]{2,1,0:T(8,128)(2,1)S(1)}, bf16[4,1104,384]{2,1,0:T(8,128)(2,1)S(1)}, u32[]{:S(2)}, u32[]{:S(2)}) %collective-permute-start.3) | collective-permute-done | bytes 3391520 | tf_op jit(solution)/shard_map/ppermute | solution.py:339
  63.9 4.0 %shard_map.75 = bf16[4,208,128]{2,1,0:T(8,128)(2,1)S(1)} custom-call(s32[10]{0:T(128)S(1)} %copy-done.1, bf16[128,384]{1,0:T(8,128)(2,1)} %copy-done.4, bf16[128,384]{1,0:T(8,128)(2,1)} %copy-done.2, bf16[128,384]{1,0:T(8,128)(2,1)} %copy-done.3, bf16[128,384]{1,0:T(8,128)(2,1)} %copy-done.2, bf16[4,1104,384]{2,1,0:T(8,128)(2,1)S(1)} %collective-permute-done.3.theirs_ref, ...), custom_call_target="tpu_custom_call" | custom-call | flops 805306368 | bytes 3145728 | tf_op jit(solution)/shard_map/pallas_call | solution.py:265
  68.0 0.0 copy-start
  68.0 13.2 %collective-permute-start.7 = (bf16[4,208,128]{2,1,0:T(8,128)(2,1)S(1)}, bf16[4,208,128]{2,1,0:T(8,128)(2,1)S(1)}, u32[]{:S(2)}, u32[]{:S(2)}) collective-permute-start(bf16[4,208,128]{2,1,0:T(8,128)(2,1)S(1)} %shard_map.75), channel_id=1, source_target_pairs={{0,8},{8,0},{1,9},{9,1},{2,10},{10,2},{3,11},{11,3},{4,12},{12,4},... | collective-permute-start | bytes 638984 | tf_op jit(solution)/shard_map/ppermute | solution.py:274
  81.2 0.0 copy-done.8
  81.2 1.9 %collective-permute-start.4 = (bf16[128,384]{1,0:T(8,128)(2,1)S(1)}, bf16[128,384]{1,0:T(8,128)(2,1)S(1)}, u32[]{:S(2)}, u32[]{:S(2)}) collective-permute-start(bf16[128,384]{1,0:T(8,128)(2,1)S(1)} %copy-done.8), channel_id=1, source_target_pairs={{0,16},{16,32},{32,48},{48,0},{1,17},{17,33},{33,49},{49,1},{2,18}... | collective-permute-start | bytes 294920 | tf_op jit(solution)/shard_map/ppermute | solution.py:276
  83.1 0.0 copy-done.7
  83.1 4.0 %collective-permute-start.5 = (bf16[128,384]{1,0:T(8,128)(2,1)S(1)}, bf16[128,384]{1,0:T(8,128)(2,1)S(1)}, u32[]{:S(2)}, u32[]{:S(2)}) collective-permute-start(bf16[128,384]{1,0:T(8,128)(2,1)S(1)} %copy-done.7), channel_id=1, source_target_pairs={{0,32},{16,48},{32,0},{48,16},{1,33},{17,49},{33,1},{49,17},{2,34}... | collective-permute-start | bytes 294920 | tf_op jit(solution)/shard_map/ppermute | solution.py:276
  87.1 0.0 copy-done.6
  87.1 3.1 %collective-permute-start.6 = (bf16[128,384]{1,0:T(8,128)(2,1)S(1)}, bf16[128,384]{1,0:T(8,128)(2,1)S(1)}, u32[]{:S(2)}, u32[]{:S(2)}) collective-permute-start(bf16[128,384]{1,0:T(8,128)(2,1)S(1)} %copy-done.6), channel_id=1, source_target_pairs={{0,48},{16,0},{32,16},{48,32},{1,49},{17,1},{33,17},{49,33},{2,50}... | collective-permute-start | bytes 294920 | tf_op jit(solution)/shard_map/ppermute | solution.py:276
  90.2 6.4 %shard_map.76 = (f32[3,4,64,128]{3,2,1,0:T(8,128)S(1)}, f32[3,4,64,256]{3,2,1,0:T(8,128)S(1)}) custom-call(s32[10]{0:T(128)S(1)} %copy-done.1, bf16[4,1104,384]{2,1,0:T(8,128)(2,1)S(1)} %all-to-all-done.mine_ref.q_ref, bf16[4,1104,384]{2,1,0:T(8,128)(2,1)S(1)} %collective-permute-done.3.theirs_ref), custom_call_target="tpu_custom_call" | custom-call | flops 1610612736 | bytes 6291456 | tf_op jit(solution)/shard_map/pallas_call | solution.py:281
  96.6 0.0 copy-start.5
  96.7 0.0 collective-permute-done.4.o1
  96.7 0.0 collective-permute-done.5.o2
  96.7 0.0 collective-permute-done.6.o3
  96.7 0.0 copy-done
  96.7 3.3 %shard_map.77 = (f32[3,4,64,128]{3,2,1,0:T(8,128)S(1)}, f32[3,4,64,128]{3,2,1,0:T(8,128)S(1)}) custom-call(s32[10]{0:T(128)S(1)} %copy-done.1, bf16[4,1104,384]{2,1,0:T(8,128)(2,1)S(1)} %all-to-all-done.mine_ref.q_ref, bf16[128,384]{1,0:T(8,128)(2,1)S(1)} %copy-done, bf16[128,384]{1,0:T(8,128)(2,1)S(1)} %collective-permute-done.4.o1, ...), custom_call_target="tpu_custom_call" | custom-call | tf_op jit(solution)/shard_map/pallas_call | solution.py:296
  100.0 0.0 collective-permute-done.7.far_ref
  100.0 1.0 shard_map.78
  101.0 6.9 %all-to-all-start.1 = ((bf16[16,48,128]{2,1,0:T(8,128)(2,1)}), bf16[16,48,128]{2,1,0:T(8,128)(2,1)S(1)}, u32[]{:S(2)}, u32[]{:S(2)}) async-start(bf16[16,48,128]{2,1,0:T(8,128)(2,1)} %shard_map.78), calls=%async_computation.1 | async-start | bytes 393216 | tf_op jit(solution)/shard_map/all_to_all | solution.py:341
  107.9 0.0 copy-done.5
  108.0 8.0 %all-to-all-done.1.part_ref = bf16[16,48,128]{2,1,0:T(8,128)(2,1)S(1)} async-done(((bf16[16,48,128]{2,1,0:T(8,128)(2,1)}), bf16[16,48,128]{2,1,0:T(8,128)(2,1)S(1)}, u32[]{:S(2)}, u32[]{:S(2)}) %all-to-all-start.1) | async-done | bytes 196640 | tf_op jit(solution)/shard_map/all_to_all | solution.py:341
  116.0 0.8 shard_map.79
  (4 shorter events, 0.0 us)
Async XLA Ops:
  5.4 22.2 %copy-start.9 = (bf16[128,384]{1,0:T(8,128)(2,1)S(1)}, bf16[128,384]{1,0:T(8,128)(2,1)}, u32[]{:S(2)}) copy-start(bf16[128,384]{1,0:T(8,128)(2,1)} %get-tuple-element.28) | copy-start | bytes 294916
  5.4 52.5 %copy-start.1 = (s32[10]{0:T(128)S(1)}, s32[10]{0:T(128)}, u32[]{:S(2)}) copy-start(s32[10]{0:T(128)} %stack.40.place_ref) | copy-start | bytes 124
  5.4 50.6 %all-to-all-start = ((bf16[4,1104,384]{2,1,0:T(8,128)(2,1)}), bf16[4,1104,384]{2,1,0:T(8,128)(2,1)S(1)}, u32[]{:S(2)}, u32[]{:S(2)}) async-start(bf16[4,1104,384]{2,1,0:T(8,128)(2,1)} %get-tuple-element.27), calls=%async_computation | async-start | bytes 6782976 | tf_op jit(solution)/shard_map/all_to_all | solution.py:327
  9.9 33.1 %collective-permute-start.1 = (bf16[128,384]{1,0:T(8,128)(2,1)}, bf16[128,384]{1,0:T(8,128)(2,1)S(1)}, u32[]{:S(2)}, u32[]{:S(2)}) collective-permute-start(bf16[128,384]{1,0:T(8,128)(2,1)} %get-tuple-element.29), channel_id=1, source_target_pairs={{0,40},{8,32},{16,56},{24,48},{32,8},{40,0},{48,24},{56,16},{1,41}... | collective-permute-start | bytes 294920 | tf_op jit(solution)/shard_map/ppermute | solution.py:331
  27.6 20.6 %collective-permute-start = (bf16[128,384]{1,0:T(8,128)(2,1)S(1)}, bf16[128,384]{1,0:T(8,128)(2,1)S(1)}, u32[]{:S(2)}, u32[]{:S(2)}) collective-permute-start(bf16[128,384]{1,0:T(8,128)(2,1)S(1)} %copy-done.9), channel_id=1, source_target_pairs={{0,8},{8,0},{16,24},{24,16},{32,40},{40,32},{48,56},{56,48},{1,9},... | collective-permute-start | bytes 294920 | tf_op jit(solution)/shard_map/ppermute | solution.py:331
  43.0 7.8 %copy-start.3 = (bf16[128,384]{1,0:T(8,128)(2,1)}, bf16[128,384]{1,0:T(8,128)(2,1)S(1)}, u32[]{:S(2)}) copy-start(bf16[128,384]{1,0:T(8,128)(2,1)S(1)} %collective-permute-done.1.f2) | copy-start | bytes 294916
  48.3 2.5 %copy-start.4 = (bf16[128,384]{1,0:T(8,128)(2,1)}, bf16[128,384]{1,0:T(8,128)(2,1)S(1)}, u32[]{:S(2)}) copy-start(bf16[128,384]{1,0:T(8,128)(2,1)S(1)} %collective-permute-done.f0) | copy-start | bytes 294916
  48.3 7.7 %collective-permute-start.2 = (bf16[128,384]{1,0:T(8,128)(2,1)S(1)}, bf16[128,384]{1,0:T(8,128)(2,1)S(1)}, u32[]{:S(2)}, u32[]{:S(2)}) collective-permute-start(bf16[128,384]{1,0:T(8,128)(2,1)S(1)} %pad_maximum_fusion), channel_id=1, source_target_pairs={{0,16},{16,32},{32,48},{48,0},{1,17},{17,33},{33,49},{49,1},{2,18}... | collective-permute-start | bytes 294920 | tf_op jit(solution)/shard_map/ppermute | solution.py:335
  56.0 1.9 %copy-start.2 = (bf16[128,384]{1,0:T(8,128)(2,1)}, bf16[128,384]{1,0:T(8,128)(2,1)S(1)}, u32[]{:S(2)}) copy-start(bf16[128,384]{1,0:T(8,128)(2,1)S(1)} %collective-permute-done.2.f1.f3) | copy-start | bytes 294916
  56.0 7.9 %collective-permute-start.3 = (bf16[4,1104,384]{2,1,0:T(8,128)(2,1)S(1)}, bf16[4,1104,384]{2,1,0:T(8,128)(2,1)S(1)}, u32[]{:S(2)}, u32[]{:S(2)}) collective-permute-start(bf16[4,1104,384]{2,1,0:T(8,128)(2,1)S(1)} %all-to-all-done.mine_ref.q_ref), channel_id=1, source_target_pairs={{0,4},{4,0},{1,5},{5,1},{2,6},{6,2},{3,7},{7,3},{8,12},{12,8},{9,1... | collective-permute-start | bytes 10174472 | tf_op jit(solution)/shard_map/ppermute | solution.py:339
  61.9 19.3 %copy-start.8 = (bf16[128,384]{1,0:T(8,128)(2,1)S(1)}, bf16[128,384]{1,0:T(8,128)(2,1)}, u32[]{:S(2)}) copy-start(bf16[128,384]{1,0:T(8,128)(2,1)} %get-tuple-element.41) | copy-start | bytes 294916
  61.9 21.2 %copy-start.7 = (bf16[128,384]{1,0:T(8,128)(2,1)S(1)}, bf16[128,384]{1,0:T(8,128)(2,1)}, u32[]{:S(2)}) copy-start(bf16[128,384]{1,0:T(8,128)(2,1)} %get-tuple-element.42) | copy-start | bytes 294916
  61.9 25.2 %copy-start.6 = (bf16[128,384]{1,0:T(8,128)(2,1)S(1)}, bf16[128,384]{1,0:T(8,128)(2,1)}, u32[]{:S(2)}) copy-start(bf16[128,384]{1,0:T(8,128)(2,1)} %get-tuple-element.43) | copy-start | bytes 294916
  68.0 28.7 %copy-start = (bf16[128,384]{1,0:T(8,128)(2,1)S(1)}, bf16[128,384]{1,0:T(8,128)(2,1)}, u32[]{:S(2)}) copy-start(bf16[128,384]{1,0:T(8,128)(2,1)} %get-tuple-element.40.o0) | copy-start | bytes 294916
  68.0 32.1 %collective-permute-start.7 = (bf16[4,208,128]{2,1,0:T(8,128)(2,1)S(1)}, bf16[4,208,128]{2,1,0:T(8,128)(2,1)S(1)}, u32[]{:S(2)}, u32[]{:S(2)}) collective-permute-start(bf16[4,208,128]{2,1,0:T(8,128)(2,1)S(1)} %shard_map.75), channel_id=1, source_target_pairs={{0,8},{8,0},{1,9},{9,1},{2,10},{10,2},{3,11},{11,3},{4,12},{12,4},... | collective-permute-start | bytes 638984 | tf_op jit(solution)/shard_map/ppermute | solution.py:274
  81.2 15.5 %collective-permute-start.4 = (bf16[128,384]{1,0:T(8,128)(2,1)S(1)}, bf16[128,384]{1,0:T(8,128)(2,1)S(1)}, u32[]{:S(2)}, u32[]{:S(2)}) collective-permute-start(bf16[128,384]{1,0:T(8,128)(2,1)S(1)} %copy-done.8), channel_id=1, source_target_pairs={{0,16},{16,32},{32,48},{48,0},{1,17},{17,33},{33,49},{49,1},{2,18}... | collective-permute-start | bytes 294920 | tf_op jit(solution)/shard_map/ppermute | solution.py:276
  83.1 13.6 %collective-permute-start.5 = (bf16[128,384]{1,0:T(8,128)(2,1)S(1)}, bf16[128,384]{1,0:T(8,128)(2,1)S(1)}, u32[]{:S(2)}, u32[]{:S(2)}) collective-permute-start(bf16[128,384]{1,0:T(8,128)(2,1)S(1)} %copy-done.7), channel_id=1, source_target_pairs={{0,32},{16,48},{32,0},{48,16},{1,33},{17,49},{33,1},{49,17},{2,34}... | collective-permute-start | bytes 294920 | tf_op jit(solution)/shard_map/ppermute | solution.py:276
  87.1 9.6 %collective-permute-start.6 = (bf16[128,384]{1,0:T(8,128)(2,1)S(1)}, bf16[128,384]{1,0:T(8,128)(2,1)S(1)}, u32[]{:S(2)}, u32[]{:S(2)}) collective-permute-start(bf16[128,384]{1,0:T(8,128)(2,1)S(1)} %copy-done.6), channel_id=1, source_target_pairs={{0,48},{16,0},{32,16},{48,32},{1,49},{17,1},{33,17},{49,33},{2,50}... | collective-permute-start | bytes 294920 | tf_op jit(solution)/shard_map/ppermute | solution.py:276
  96.6 11.3 %copy-start.5 = (bf16[6144]{0:T(1024)(128)(2,1)S(1)}, bf16[6144]{0:T(1024)(128)(2,1)}, u32[]{:S(2)}) copy-start(bf16[6144]{0:T(1024)(128)(2,1)} %param.13) | copy-start | bytes 36868
  101.0 15.0 %all-to-all-start.1 = ((bf16[16,48,128]{2,1,0:T(8,128)(2,1)}), bf16[16,48,128]{2,1,0:T(8,128)(2,1)S(1)}, u32[]{:S(2)}, u32[]{:S(2)}) async-start(bf16[16,48,128]{2,1,0:T(8,128)(2,1)} %shard_map.78), calls=%async_computation.1 | async-start | bytes 393216 | tf_op jit(solution)/shard_map/all_to_all | solution.py:341

commit v3 on v2

--- a/solution.py
+++ b/solution.py
@@ -270,11 +270,10 @@
         scratch_shapes=[pltpu.VMEM((heads, 4, Q_ROWS, HEAD_DIM), jnp.float32), hidden],
         **common(2048),
     )(place, *far, theirs, top, total)
-    far_out, own = lax.optimization_barrier((far_out, own))
+    far_out, own[1], own[2] = lax.optimization_barrier((far_out, own[1], own[2]))
     far_out = lax.ppermute(far_out, "z", [(0, 1), (1, 0)])
-    own = [own[0]] + [
-        lax.ppermute(own[turn], "x", [(x, (x + turn) % 4) for x in range(4)]) for turn in range(1, 4)
-    ]
+    for turn in (1, 2):
+        own[turn] = lax.ppermute(own[turn], "x", [(x, (x + turn) % 4) for x in range(4)])
     near = [
         pl.BlockSpec((1, 4, Q_ROWS, width), lambda j: (j, 0, 0, 0)) for width in (HEAD_DIM, 2 * HEAD_DIM)
     ]
@@ -333,7 +332,8 @@
     far = [send(blocks[0], 0), send(blocks[1], 2)]
     odd = jnp.concatenate([block[Q_ROWS:] for block in far], 0)
     odd = lax.ppermute(odd, "x", [(x, (x + 1) % 4) for x in range(4)])
-    mine, far = lax.optimization_barrier((mine, [far[0], odd, far[1]]))
+    own[3] = lax.ppermute(own[3], "x", [(x, (x + 3) % 4) for x in range(4)])
+    mine, far, own[3] = lax.optimization_barrier((mine, [far[0], odd, far[1]], own[3]))
     far = [pltpu.with_memory_space_constraint(a, pltpu.HBM) for a in far]
     far.append(far[1])
     theirs = lax.ppermute(mine, "core", [(0, 1), (1, 0)])

time: 118 us -> 115 us (0.975)
  starting transfers between devices: 57.6 us -> 55.5 us
    ppermute x3 -> x2, starting transfers between devices: 8.97 us -> 5.89 us  [attend(): lax.ppermute(own[turn], 'x', [(x, (x + turn) % 4) for x in range(4)])]
    ppermute x0 -> x1, starting transfers between devices: none -> 3.08 us  [local(): own[3] = lax.ppermute(own[3], 'x', [(x, (x + 3) % 4) for x in range(4)])]
    ppermute x2, waiting for transfers between devices: 18.7 us -> 15.8 us  [send(): return lax.ppermute(block, ('x', 'z'), route)]
    ppermute x1, waiting for transfers between devices: 0.01 us -> 2.48 us  [attend(): far_out = lax.ppermute(far_out, 'z', [(0, 1), (1, 0)])]
    ppermute x0 -> x1, waiting for transfers between devices: none -> 1.78 us  [local(): own[3] = lax.ppermute(own[3], 'x', [(x, (x + 3) % 4) for x in range(4)])]
    all_to_all x1, starting transfers between devices: 6.91 us -> 5.14 us  [local(): block = lax.all_to_all(block, ('x', 'head'), 0, 0, tiled=True)]
    ppermute x1, waiting for transfers between devices: 5.22 us -> 3.56 us  [local(): odd = lax.ppermute(odd, 'x', [(x, (x + 1) % 4) for x in range(4)])]
  transfers between devices with their start and end apart: 10 -> 10, of which waited for: 5 -> 7; matrix products, arithmetic and copies ran while one was open for 0% -> 0% of each run, Pallas kernels for 12% -> 12%
where the time goes in v3:
time: 115 us; the launch traced here: 114 us
  starting transfers between devices  55.5 us (48%)
  waiting for transfers between devices  33.7 us (29%)
  Pallas kernels  24.2 us (21%)
    ppermute x2, starting transfers between devices, send(): return lax.ppermute(block, ('x', 'z'), route)  19.7 us
    ppermute x2, waiting for transfers between devices, send(): return lax.ppermute(block, ('x', 'z'), route)  15.8 us
    ppermute x1, starting transfers between devices, attend(): far_out = lax.ppermute(far_out, 'z', [(0, 1), (1, 0)])  13 us
    all_to_all x1, waiting for transfers between devices, local(): block = lax.all_to_all(block, ('x', 'head'), 0, 0, tiled=True)  8.04 us
    pallas_call x1, Pallas kernels, attend(): pl.pallas_call(near_kernel, in_specs=[SMEM, cache, cache], out_specs=near...  6.44 us
    ppermute x2, starting transfers between devices, attend(): lax.ppermute(own[turn], 'x', [(x, (x + turn) % 4) for x in range(4)])  5.89 us
    all_to_all x1, starting transfers between devices, local(): block = lax.all_to_all(block, ('x', 'head'), 0, 0, tiled=True)  5.14 us
    pallas_call x1, Pallas kernels, pack(): pl.pallas_call(pack_kernel, grid=(4,), in_specs=[SMEM, big, big, pl.Block...  4.71 us
  transfers between devices with their start and end apart: 10, of which 7 were waited for; matrix products, arithmetic and copies ran while one was open for 0% of the time, Pallas kernels for 12%

profile of v3, /device:TPU:32, one launch (start us, length us, event | category | flops | bytes accessed | tf_op | source)
XLA Modules:
  0.0 114.3 jit_solution(13953470952930940327)
XLA Ops:
  0.0 0.6 stack.40.place_ref
  0.6 4.7 %shard_map.73 = (bf16[4,1104,384]{2,1,0:T(8,128)(2,1)}, bf16[128,384]{1,0:T(8,128)(2,1)}, bf16[128,384]{1,0:T(8,128)(2,1)}, bf16[128,384]{1,0:T(8,128)(2,1)}, bf...) custom-call(s32[10]{0:T(128)} %stack.40.place_ref, bf16[512,1536]{1,0:T(8,128)(2,1)} %k_ref.1, ...), custom_call_target="tpu_custom_call" | custom-call | tf_op jit(solution)/shard_map/pallas_call | solution.py:71
  5.3 0.0 copy-start.1
  5.3 4.3 %all-to-all-start = ((bf16[4,1104,384]{2,1,0:T(8,128)(2,1)}), bf16[4,1104,384]{2,1,0:T(8,128)(2,1)S(1)}, u32[]{:S(2)}, u32[]{:S(2)}) async-start(bf16[4,1104,384]{2,1,0:T(8,128)(2,1)} %get-tuple-element.26), calls=%async_computation | async-start | bytes 6782976 | tf_op jit(solution)/shard_map/all_to_all | solution.py:326
  9.6 17.8 %collective-permute-start.1 = (bf16[128,384]{1,0:T(8,128)(2,1)}, bf16[128,384]{1,0:T(8,128)(2,1)S(1)}, u32[]{:S(2)}, u32[]{:S(2)}) collective-permute-start(bf16[128,384]{1,0:T(8,128)(2,1)} %get-tuple-element.28), channel_id=1, source_target_pairs={{0,40},{8,32},{16,56},{24,48},{32,8},{40,0},{48,24},{56,16},{1,41}... | collective-permute-start | bytes 294920 | tf_op jit(solution)/shard_map/ppermute | solution.py:330
  27.4 1.9 %collective-permute-start = (bf16[128,384]{1,0:T(8,128)(2,1)}, bf16[128,384]{1,0:T(8,128)(2,1)S(1)}, u32[]{:S(2)}, u32[]{:S(2)}) collective-permute-start(bf16[128,384]{1,0:T(8,128)(2,1)} %get-tuple-element.27), channel_id=1, source_target_pairs={{0,8},{8,0},{16,24},{24,16},{32,40},{40,32},{48,56},{56,48},{1,9},... | collective-permute-start | bytes 294920 | tf_op jit(solution)/shard_map/ppermute | solution.py:330
  29.3 3.1 %collective-permute-start.3 = (bf16[128,384]{1,0:T(8,128)(2,1)}, bf16[128,384]{1,0:T(8,128)(2,1)S(1)}, u32[]{:S(2)}, u32[]{:S(2)}) collective-permute-start(bf16[128,384]{1,0:T(8,128)(2,1)} %get-tuple-element.29), channel_id=1, source_target_pairs={{0,48},{16,0},{32,16},{48,32},{1,49},{17,1},{33,17},{49,33},{2,50}... | collective-permute-start | bytes 294920 | tf_op jit(solution)/shard_map/ppermute | solution.py:335
  32.4 10.3 %collective-permute-done.1.f2 = bf16[128,384]{1,0:T(8,128)(2,1)S(1)} collective-permute-done((bf16[128,384]{1,0:T(8,128)(2,1)}, bf16[128,384]{1,0:T(8,128)(2,1)S(1)}, u32[]{:S(2)}, u32[]{:S(2)}) %collective-permute-start.1) | collective-permute-done | bytes 98336 | tf_op jit(solution)/shard_map/ppermute | solution.py:330
  42.8 0.0 copy-start.2
  42.8 5.5 %collective-permute-done.f0 = bf16[128,384]{1,0:T(8,128)(2,1)S(1)} collective-permute-done((bf16[128,384]{1,0:T(8,128)(2,1)}, bf16[128,384]{1,0:T(8,128)(2,1)S(1)}, u32[]{:S(2)}, u32[]{:S(2)}) %collective-permute-start) | collective-permute-done | bytes 98336 | tf_op jit(solution)/shard_map/ppermute | solution.py:330
  48.2 0.0 copy-start.3
  48.3 2.5 %collective-permute-start.2 = (bf16[128,384]{1,0:T(8,128)(2,1)S(1)}, bf16[128,384]{1,0:T(8,128)(2,1)}, u32[]{:S(2)}, u32[]{:S(2)}) collective-permute-start(bf16[128,384]{1,0:T(8,128)(2,1)S(1)} %pad_maximum_fusion), channel_id=1, source_target_pairs={{0,16},{16,32},{32,48},{48,0},{1,17},{17,33},{33,49},{49,1},{2,18}... | collective-permute-start | bytes 294920 | tf_op jit(solution)/shard_map/ppermute | solution.py:334
  50.8 1.8 %collective-permute-done.3.o3 = bf16[128,384]{1,0:T(8,128)(2,1)S(1)} collective-permute-done((bf16[128,384]{1,0:T(8,128)(2,1)}, bf16[128,384]{1,0:T(8,128)(2,1)S(1)}, u32[]{:S(2)}, u32[]{:S(2)}) %collective-permute-start.3) | collective-permute-done | bytes 98336 | tf_op jit(solution)/shard_map/ppermute | solution.py:335
  52.5 0.0 copy-done.2
  52.5 0.0 copy-done.3
  52.5 3.6 %collective-permute-done.2.f1.f3 = bf16[128,384]{1,0:T(8,128)(2,1)} collective-permute-done((bf16[128,384]{1,0:T(8,128)(2,1)S(1)}, bf16[128,384]{1,0:T(8,128)(2,1)}, u32[]{:S(2)}, u32[]{:S(2)}) %collective-permute-start.2) | collective-permute-done | bytes 98336 | tf_op jit(solution)/shard_map/ppermute | solution.py:334
  56.1 0.0 all-to-all-done.mine_ref.q_ref
  56.1 1.9 %collective-permute-start.4 = (bf16[4,1104,384]{2,1,0:T(8,128)(2,1)S(1)}, bf16[4,1104,384]{2,1,0:T(8,128)(2,1)S(1)}, u32[]{:S(2)}, u32[]{:S(2)}) collective-permute-start(bf16[4,1104,384]{2,1,0:T(8,128)(2,1)S(1)} %all-to-all-done.mine_ref.q_ref), channel_id=1, source_target_pairs={{0,4},{4,0},{1,5},{5,1},{2,6},{6,2},{3,7},{7,3},{8,12},{12,8},{9,1... | collective-permute-start | bytes 10174472 | tf_op jit(solution)/shard_map/ppermute | solution.py:339
  58.0 0.0 copy-done.1
  58.0 3.9 %shard_map.74 = (f32[3,256,128]{2,1,0:T(8,128)S(1)}, f32[3,256,256]{2,1,0:T(8,128)S(1)}) custom-call(s32[10]{0:T(128)S(1)} %copy-done.1, bf16[128,384]{1,0:T(8,128)(2,1)} %copy-done.3, bf16[128,384]{1,0:T(8,128)(2,1)} %collective-permute-done.2.f1.f3, bf16[128,384]{1,0:T(8,128)(2,1)} %copy-done.2, bf16[128,384]{1,0:T(8,128)(2,1)} %collective-permute-done.2.f1.f3, ...), custom_call_target="tpu_custom_call" | custom-call | flops 805306368 | bytes 3145728 | tf_op jit(solution)/shard_map/pallas_call | solution.py:257
  62.0 0.0 copy-start.6
  62.0 0.0 copy-start.5
  62.0 2.0 %collective-permute-done.4.theirs_ref = bf16[4,1104,384]{2,1,0:T(8,128)(2,1)S(1)} collective-permute-done((bf16[4,1104,384]{2,1,0:T(8,128)(2,1)S(1)}, bf16[4,1104,384]{2,1,0:T(8,128)(2,1)S(1)}, u32[]{:S(2)}, u32[]{:S(2)}) %collective-permute-start.4) | collective-permute-done | bytes 3391520 | tf_op jit(solution)/shard_map/ppermute | solution.py:339
  64.0 4.0 %shard_map.75 = bf16[4,208,128]{2,1,0:T(8,128)(2,1)S(1)} custom-call(s32[10]{0:T(128)S(1)} %copy-done.1, bf16[128,384]{1,0:T(8,128)(2,1)} %copy-done.3, bf16[128,384]{1,0:T(8,128)(2,1)} %collective-permute-done.2.f1.f3, bf16[128,384]{1,0:T(8,128)(2,1)} %copy-done.2, bf16[128,384]{1,0:T(8,128)(2,1)} %collective-permute-done.2.f1.f3, ...), custom_call_target="tpu_custom_call" | custom-call | flops 805306368 | bytes 3145728 | tf_op jit(solution)/shard_map/pallas_call | solution.py:265
  68.0 0.0 copy-start
  68.0 13.0 %collective-permute-start.7 = (bf16[4,208,128]{2,1,0:T(8,128)(2,1)S(1)}, bf16[4,208,128]{2,1,0:T(8,128)(2,1)S(1)}, u32[]{:S(2)}, u32[]{:S(2)}) collective-permute-start(bf16[4,208,128]{2,1,0:T(8,128)(2,1)S(1)} %shard_map.75), channel_id=1, source_target_pairs={{0,8},{8,0},{1,9},{9,1},{2,10},{10,2},{3,11},{11,3},{4,12},{12,4},... | collective-permute-start | bytes 638984 | tf_op jit(solution)/shard_map/ppermute | solution.py:274
  81.0 0.0 copy-done.6
  81.1 1.9 %collective-permute-start.5 = (bf16[128,384]{1,0:T(8,128)(2,1)S(1)}, bf16[128,384]{1,0:T(8,128)(2,1)S(1)}, u32[]{:S(2)}, u32[]{:S(2)}) collective-permute-start(bf16[128,384]{1,0:T(8,128)(2,1)S(1)} %copy-done.6), channel_id=1, source_target_pairs={{0,16},{16,32},{32,48},{48,0},{1,17},{17,33},{33,49},{49,1},{2,18}... | collective-permute-start | bytes 294920 | tf_op jit(solution)/shard_map/ppermute | solution.py:276
  83.0 0.0 copy-done.5
  83.0 4.0 %collective-permute-start.6 = (bf16[128,384]{1,0:T(8,128)(2,1)S(1)}, bf16[128,384]{1,0:T(8,128)(2,1)S(1)}, u32[]{:S(2)}, u32[]{:S(2)}) collective-permute-start(bf16[128,384]{1,0:T(8,128)(2,1)S(1)} %copy-done.5), channel_id=1, source_target_pairs={{0,32},{16,48},{32,0},{48,16},{1,33},{17,49},{33,1},{49,17},{2,34}... | collective-permute-start | bytes 294920 | tf_op jit(solution)/shard_map/ppermute | solution.py:276
  87.0 6.4 %shard_map.76 = (f32[3,4,64,128]{3,2,1,0:T(8,128)S(1)}, f32[3,4,64,256]{3,2,1,0:T(8,128)S(1)}) custom-call(s32[10]{0:T(128)S(1)} %copy-done.1, bf16[4,1104,384]{2,1,0:T(8,128)(2,1)S(1)} %all-to-all-done.mine_ref.q_ref, bf16[4,1104,384]{2,1,0:T(8,128)(2,1)S(1)} %collective-permute-done.4.theirs_ref), custom_call_target="tpu_custom_call" | custom-call | flops 1610612736 | bytes 6291456 | tf_op jit(solution)/shard_map/pallas_call | solution.py:280
  93.4 0.0 copy-start.4
  93.4 0.0 collective-permute-done.5.o1
  93.4 0.0 collective-permute-done.6.o2
  93.5 0.0 copy-done
  93.5 3.3 %shard_map.77 = (f32[3,4,64,128]{3,2,1,0:T(8,128)S(1)}, f32[3,4,64,128]{3,2,1,0:T(8,128)S(1)}) custom-call(s32[10]{0:T(128)S(1)} %copy-done.1, bf16[4,1104,384]{2,1,0:T(8,128)(2,1)S(1)} %all-to-all-done.mine_ref.q_ref, bf16[128,384]{1,0:T(8,128)(2,1)S(1)} %copy-done, bf16[128,384]{1,0:T(8,128)(2,1)S(1)} %collective-permute-done.5.o1, ...), custom_call_target="tpu_custom_call" | custom-call | tf_op jit(solution)/shard_map/pallas_call | solution.py:295
  96.8 2.5 %collective-permute-done.7.far_ref = bf16[4,208,128]{2,1,0:T(8,128)(2,1)S(1)} collective-permute-done((bf16[4,208,128]{2,1,0:T(8,128)(2,1)S(1)}, bf16[4,208,128]{2,1,0:T(8,128)(2,1)S(1)}, u32[]{:S(2)}, u32[]{:S(2)}) %collective-permute-start.7) | collective-permute-done | bytes 213024 | tf_op jit(solution)/shard_map/ppermute | solution.py:274
  99.3 1.0 shard_map.78
  100.2 5.1 %all-to-all-start.1 = ((bf16[16,48,128]{2,1,0:T(8,128)(2,1)}), bf16[16,48,128]{2,1,0:T(8,128)(2,1)S(1)}, u32[]{:S(2)}, u32[]{:S(2)}) async-start(bf16[16,48,128]{2,1,0:T(8,128)(2,1)} %shard_map.78), calls=%async_computation.1 | async-start | bytes 393216 | tf_op jit(solution)/shard_map/all_to_all | solution.py:341
  105.4 0.0 copy-done.4
  105.4 8.0 %all-to-all-done.1.part_ref = bf16[16,48,128]{2,1,0:T(8,128)(2,1)S(1)} async-done(((bf16[16,48,128]{2,1,0:T(8,128)(2,1)}), bf16[16,48,128]{2,1,0:T(8,128)(2,1)S(1)}, u32[]{:S(2)}, u32[]{:S(2)}) %all-to-all-start.1) | async-done | bytes 196640 | tf_op jit(solution)/shard_map/all_to_all | solution.py:341
  113.5 0.8 shard_map.79
  (4 shorter events, 0.0 us)
Async XLA Ops:
  5.3 52.7 %copy-start.1 = (s32[10]{0:T(128)S(1)}, s32[10]{0:T(128)}, u32[]{:S(2)}) copy-start(s32[10]{0:T(128)} %stack.40.place_ref) | copy-start | bytes 124
  5.3 50.8 %all-to-all-start = ((bf16[4,1104,384]{2,1,0:T(8,128)(2,1)}), bf16[4,1104,384]{2,1,0:T(8,128)(2,1)S(1)}, u32[]{:S(2)}, u32[]{:S(2)}) async-start(bf16[4,1104,384]{2,1,0:T(8,128)(2,1)} %get-tuple-element.26), calls=%async_computation | async-start | bytes 6782976 | tf_op jit(solution)/shard_map/all_to_all | solution.py:326
  9.6 33.1 %collective-permute-start.1 = (bf16[128,384]{1,0:T(8,128)(2,1)}, bf16[128,384]{1,0:T(8,128)(2,1)S(1)}, u32[]{:S(2)}, u32[]{:S(2)}) collective-permute-start(bf16[128,384]{1,0:T(8,128)(2,1)} %get-tuple-element.28), channel_id=1, source_target_pairs={{0,40},{8,32},{16,56},{24,48},{32,8},{40,0},{48,24},{56,16},{1,41}... | collective-permute-start | bytes 294920 | tf_op jit(solution)/shard_map/ppermute | solution.py:330
  27.4 20.8 %collective-permute-start = (bf16[128,384]{1,0:T(8,128)(2,1)}, bf16[128,384]{1,0:T(8,128)(2,1)S(1)}, u32[]{:S(2)}, u32[]{:S(2)}) collective-permute-start(bf16[128,384]{1,0:T(8,128)(2,1)} %get-tuple-element.27), channel_id=1, source_target_pairs={{0,8},{8,0},{16,24},{24,16},{32,40},{40,32},{48,56},{56,48},{1,9},... | collective-permute-start | bytes 294920 | tf_op jit(solution)/shard_map/ppermute | solution.py:330
  29.3 23.2 %collective-permute-start.3 = (bf16[128,384]{1,0:T(8,128)(2,1)}, bf16[128,384]{1,0:T(8,128)(2,1)S(1)}, u32[]{:S(2)}, u32[]{:S(2)}) collective-permute-start(bf16[128,384]{1,0:T(8,128)(2,1)} %get-tuple-element.29), channel_id=1, source_target_pairs={{0,48},{16,0},{32,16},{48,32},{1,49},{17,1},{33,17},{49,33},{2,50}... | collective-permute-start | bytes 294920 | tf_op jit(solution)/shard_map/ppermute | solution.py:335
  42.8 9.8 %copy-start.2 = (bf16[128,384]{1,0:T(8,128)(2,1)}, bf16[128,384]{1,0:T(8,128)(2,1)S(1)}, u32[]{:S(2)}) copy-start(bf16[128,384]{1,0:T(8,128)(2,1)S(1)} %collective-permute-done.1.f2) | copy-start | bytes 294916
  48.2 4.3 %copy-start.3 = (bf16[128,384]{1,0:T(8,128)(2,1)}, bf16[128,384]{1,0:T(8,128)(2,1)S(1)}, u32[]{:S(2)}) copy-start(bf16[128,384]{1,0:T(8,128)(2,1)S(1)} %collective-permute-done.f0) | copy-start | bytes 294916
  48.3 7.8 %collective-permute-start.2 = (bf16[128,384]{1,0:T(8,128)(2,1)S(1)}, bf16[128,384]{1,0:T(8,128)(2,1)}, u32[]{:S(2)}, u32[]{:S(2)}) collective-permute-start(bf16[128,384]{1,0:T(8,128)(2,1)S(1)} %pad_maximum_fusion), channel_id=1, source_target_pairs={{0,16},{16,32},{32,48},{48,0},{1,17},{17,33},{33,49},{49,1},{2,18}... | collective-permute-start | bytes 294920 | tf_op jit(solution)/shard_map/ppermute | solution.py:334
  56.1 7.9 %collective-permute-start.4 = (bf16[4,1104,384]{2,1,0:T(8,128)(2,1)S(1)}, bf16[4,1104,384]{2,1,0:T(8,128)(2,1)S(1)}, u32[]{:S(2)}, u32[]{:S(2)}) collective-permute-start(bf16[4,1104,384]{2,1,0:T(8,128)(2,1)S(1)} %all-to-all-done.mine_ref.q_ref), channel_id=1, source_target_pairs={{0,4},{4,0},{1,5},{5,1},{2,6},{6,2},{3,7},{7,3},{8,12},{12,8},{9,1... | collective-permute-start | bytes 10174472 | tf_op jit(solution)/shard_map/ppermute | solution.py:339
  62.0 19.1 %copy-start.6 = (bf16[128,384]{1,0:T(8,128)(2,1)S(1)}, bf16[128,384]{1,0:T(8,128)(2,1)}, u32[]{:S(2)}) copy-start(bf16[128,384]{1,0:T(8,128)(2,1)} %get-tuple-element.39) | copy-start | bytes 294916
  62.0 21.0 %copy-start.5 = (bf16[128,384]{1,0:T(8,128)(2,1)S(1)}, bf16[128,384]{1,0:T(8,128)(2,1)}, u32[]{:S(2)}) copy-start(bf16[128,384]{1,0:T(8,128)(2,1)} %get-tuple-element.40) | copy-start | bytes 294916
  68.0 25.4 %copy-start = (bf16[128,384]{1,0:T(8,128)(2,1)S(1)}, bf16[128,384]{1,0:T(8,128)(2,1)}, u32[]{:S(2)}) copy-start(bf16[128,384]{1,0:T(8,128)(2,1)} %get-tuple-element.31.o0) | copy-start | bytes 294916
  68.0 31.2 %collective-permute-start.7 = (bf16[4,208,128]{2,1,0:T(8,128)(2,1)S(1)}, bf16[4,208,128]{2,1,0:T(8,128)(2,1)S(1)}, u32[]{:S(2)}, u32[]{:S(2)}) collective-permute-start(bf16[4,208,128]{2,1,0:T(8,128)(2,1)S(1)} %shard_map.75), channel_id=1, source_target_pairs={{0,8},{8,0},{1,9},{9,1},{2,10},{10,2},{3,11},{11,3},{4,12},{12,4},... | collective-permute-start | bytes 638984 | tf_op jit(solution)/shard_map/ppermute | solution.py:274
  81.1 12.4 %collective-permute-start.5 = (bf16[128,384]{1,0:T(8,128)(2,1)S(1)}, bf16[128,384]{1,0:T(8,128)(2,1)S(1)}, u32[]{:S(2)}, u32[]{:S(2)}) collective-permute-start(bf16[128,384]{1,0:T(8,128)(2,1)S(1)} %copy-done.6), channel_id=1, source_target_pairs={{0,16},{16,32},{32,48},{48,0},{1,17},{17,33},{33,49},{49,1},{2,18}... | collective-permute-start | bytes 294920 | tf_op jit(solution)/shard_map/ppermute | solution.py:276
  83.0 10.4 %collective-permute-start.6 = (bf16[128,384]{1,0:T(8,128)(2,1)S(1)}, bf16[128,384]{1,0:T(8,128)(2,1)S(1)}, u32[]{:S(2)}, u32[]{:S(2)}) collective-permute-start(bf16[128,384]{1,0:T(8,128)(2,1)S(1)} %copy-done.5), channel_id=1, source_target_pairs={{0,32},{16,48},{32,0},{48,16},{1,33},{17,49},{33,1},{49,17},{2,34}... | collective-permute-start | bytes 294920 | tf_op jit(solution)/shard_map/ppermute | solution.py:276
  93.4 12.0 %copy-start.4 = (bf16[6144]{0:T(1024)(128)(2,1)S(1)}, bf16[6144]{0:T(1024)(128)(2,1)}, u32[]{:S(2)}) copy-start(bf16[6144]{0:T(1024)(128)(2,1)} %param.13) | copy-start | bytes 36868
  100.2 13.2 %all-to-all-start.1 = ((bf16[16,48,128]{2,1,0:T(8,128)(2,1)}), bf16[16,48,128]{2,1,0:T(8,128)(2,1)S(1)}, u32[]{:S(2)}, u32[]{:S(2)}) async-start(bf16[16,48,128]{2,1,0:T(8,128)(2,1)} %shard_map.78), calls=%async_computation.1 | async-start | bytes 393216 | tf_op jit(solution)/shard_map/all_to_all | solution.py:341
